TPU v7x, 32 devices: a whole 2x2x4 slice. The times are simulated.
32 devices in a mesh: text: 16 (over z, y, core), video: 2 (over x).
Axes of the slice: x: 2, y: 2, z: 4, core: 2. Of those that a mesh axis runs over, the one named last changes fastest.
Arguments:
- queries: bfloat16 [2048, 4096], P('text'), may hold values from -53 to 53
- video_keys: bfloat16 [512, 512], P('video'), may hold values from -6 to 6
- video_values: bfloat16 [512, 512], P('video'), may hold values from -6 to 6
- grad_out: bfloat16 [2048, 4096], P('text'), may hold values from -6 to 6
- positions: int32 [2048], P('text'), may hold values from 1 to 511, as said below
- span_bounds: int32 [16, 2], P('text'), may hold values from 0 to 512, as said below
Outputs:
- attended: bfloat16 [2048, 4096], P('text', 'video')
- grad_query: bfloat16 [2048, 4096], P('text', 'video')
- grad_key: bfloat16 [512, 512], P(('video', 'text'))
- grad_value: bfloat16 [512, 512], P(('video', 'text'))
Inputs may be any that keep to these rules, and one draw needn't show every extreme that they name: `span_bounds`: column 0 is a multiple of 128 from 0 to 0; column 1 is a multiple of 128 from 512 to 512. `positions`: each position is at least its block's span start plus 1.
All inputs are finite; a program needn't handle non-finite values.
Results may differ from a plain program's by a relative error of at most 0.017.
Values sent between devices are 32-bit elements; how exact they have to be, the bound alone decides.
A program may use at most 128 MiB of HBM per device.

v0:
```python
import jax
import jax.numpy as jnp
from jax import lax
from jax.sharding import PartitionSpec as P

H = 32
G = 4
HD = 128
TBLK = 128


masked_floor = -1e30


def joined(value, axis, join):
    pieces = jax.tree.map(lambda part: lax.all_gather(part, axis), value)
    head = jax.tree.map(lambda part: part[0], pieces)
    tail = jax.tree.map(lambda part: part[1:], pieces)
    total, _ = lax.scan(lambda total, section: (join(total, section), None), head, tail)
    return total


def widen(stats):
    return jnp.repeat(stats, HD, axis=1)


def merge_blocks(first_part, second_part):
    peak_one, total_one, out_one = first_part
    peak_two, total_two, out_two = second_part
    row_top = jnp.maximum(peak_one, peak_two)
    factor_one = jnp.exp(peak_one - row_top)
    factor_two = jnp.exp(peak_two - row_top)
    return (
        row_top,
        total_one * factor_one + total_two * factor_two,
        out_one * widen(factor_one) + out_two * widen(factor_two),
    )


def local(queries, video_keys, video_values, grad_out, positions, span_bounds):
    row_count = queries.shape[0]
    video_count = video_keys.shape[0]
    per_group = H // G
    score_scale = HD ** (-0.5)
    video_rank = lax.axis_index("video")
    video_size = lax.axis_size("video")
    columns = video_rank * video_count + jnp.arange(video_count, dtype=jnp.int32)
    lower_rows = jnp.repeat(span_bounds[:, 0], TBLK, total_repeat_length=row_count)
    upper_rows = jnp.repeat(span_bounds[:, 1], TBLK, total_repeat_length=row_count)
    visible = (
        (columns[None, :] >= lower_rows[:, None])
        & (columns[None, :] < upper_rows[:, None])
        & (columns[None, :] <= positions[:, None])
    )[:, None, :]

    def group_parts(group):
        head_start = group * per_group * HD
        head_stop = (group + 1) * per_group * HD
        query_grp = queries[:, head_start:head_stop].reshape(row_count, per_group, HD)
        grad_grp = grad_out[:, head_start:head_stop].reshape(row_count, per_group, HD)
        key_grp = video_keys[:, group * HD : (group + 1) * HD]
        value_grp = video_values[:, group * HD : (group + 1) * HD]
        scores = (
            jnp.einsum("rhd,cd->rhc", query_grp, key_grp, preferred_element_type=jnp.float32)
            * score_scale
        )
        masked = jnp.where(visible, scores, masked_floor)
        return (query_grp, grad_grp, key_grp, value_grp, masked)

    peaks, totals, partial_value = ([], [], [])
    for group in range(G):
        query_grp, grad_grp, key_grp, value_grp, masked = group_parts(group)
        block_peak = jnp.max(masked, axis=2)
        weights = jnp.where(visible, jnp.exp(masked - block_peak[:, :, None]), 0.0)
        peaks.append(block_peak)
        totals.append(jnp.sum(weights, axis=2))
        partial_value.append(
            jnp.einsum(
                "rhc,cd->rhd",
                weights.astype(jnp.bfloat16),
                value_grp,
                preferred_element_type=jnp.float32,
            ).reshape(row_count, per_group * HD)
        )
    local_peak = jnp.concatenate(peaks, axis=1)
    local_total = jnp.concatenate(totals, axis=1)
    local_out = jnp.concatenate(partial_value, axis=1)
    width = H * HD // video_size
    row_top, denom, numer = joined((local_peak, local_total, local_out), "video", merge_blocks)
    attended_all = (numer / widen(denom)).astype(jnp.bfloat16)
    log_norm = row_top + jnp.log(denom)
    delta = jnp.sum(
        (grad_out.astype(jnp.float32) * attended_all.astype(jnp.float32)).reshape(row_count, H, HD),
        axis=2,
    )
    attended = lax.dynamic_slice_in_dim(attended_all, video_rank * width, width, 1)
    grads_query, grads_key, grads_value = ([], [], [])
    for group in range(G):
        query_grp, grad_grp, key_grp, value_grp, masked = group_parts(group)
        norm_grp = log_norm[:, group * per_group : (group + 1) * per_group]
        delta_grp = delta[:, group * per_group : (group + 1) * per_group]
        prob = jnp.where(visible, jnp.exp(masked - norm_grp[:, :, None]), 0.0)
        dprob = jnp.einsum("rhd,cd->rhc", grad_grp, value_grp, preferred_element_type=jnp.float32)
        dscore = (prob * (dprob - delta_grp[:, :, None])).astype(jnp.bfloat16)
        grads_query.append(
            jnp.einsum("rhc,cd->rhd", dscore, key_grp, preferred_element_type=jnp.float32).reshape(
                row_count, per_group * HD
            )
            * score_scale
        )
        grads_key.append(
            jnp.einsum("rhc,rhd->cd", dscore, query_grp, preferred_element_type=jnp.float32)
            * score_scale
        )
        grads_value.append(
            jnp.einsum(
                "rhc,rhd->cd",
                prob.astype(jnp.bfloat16),
                grad_grp,
                preferred_element_type=jnp.float32,
            )
        )
    query_terms = jnp.concatenate(grads_query, axis=1)
    key_terms = jnp.concatenate(grads_key, axis=1)
    value_terms = jnp.concatenate(grads_value, axis=1)
    grad_query = lax.psum_scatter(query_terms, "video", scatter_dimension=1, tiled=True).astype(
        jnp.bfloat16
    )
    key_sum, value_sum = (
        lax.psum_scatter(key_terms, "text", scatter_dimension=0, tiled=True),
        lax.psum_scatter(value_terms, "text", scatter_dimension=0, tiled=True),
    )
    return (attended, grad_query, key_sum.astype(jnp.bfloat16), value_sum.astype(jnp.bfloat16))


def solution(mesh):
    placed = (
        P("text", None),
        P("video", None),
        P("video", None),
        P("text", None),
        P("text"),
        P("text", None),
    )
    return jax.shard_map(
        local,
        mesh=mesh,
        in_specs=placed,
        out_specs=(
            P("text", "video"),
            P("text", "video"),
            P(("video", "text"), None),
            P(("video", "text"), None),
        ),
        check_vma=False,
    )
```

profile of v0, /device:TPU:0, one launch (start us, length us, event | category | flops | bytes accessed | tf_op | source)
XLA Modules:
  0.0 226.4 jit_solution(3736234387853890248)
XLA Ops:
  8.1 1.3 fusion.110
  9.6 0.6 fusion.113
  10.3 1.3 compare_and_fusion.1
  11.8 1.3 fusion.114
  13.1 0.4 fusion.115
  13.7 0.4 fusion.116
  14.2 0.9 copy.157
  15.1 1.4 fusion.117
  16.5 2.5 %fusion.34 = f32[128,8,128]{0,2,1:T(8,128)} fusion(f32[128,8,256]{2,0,1:T(8,128)} %get-tuple-element.107, f32[128,8]{0,1:T(8,128)S(1)} %get-tuple-element.106, pred[128,256]{1,0:T(8,128)(4,1)S(1)} %compare_and_fusion, bf16[256,512]{1,0:T(8,128)(2,1)} %param.18), kind=kOutput, calls=%fused_computation.64 | convolution fusion | flops 67895296 | bytes 1675264 | tf_op jit(solution)/shard_map/rhc,cd->rhd/dot_general | solution.py:78
  18.9 2.0 copy.99
  21.0 2.1 fusion.36
  23.0 2.0 copy.98
  25.1 2.1 fusion.38
  27.1 2.0 copy.97
  29.2 2.1 fusion.40
  31.3 2.1 copy.96
  33.3 3.1 %pad_maximum_fusion = f32[128,4096]{1,0:T(8,128)} fusion(f32[128,1024]{1,0:T(8,128)} %copy.99, f32[128,1024]{1,0:T(8,128)} %copy.98, f32[128,1024]{1,0:T(8,128)} %copy.97, f32[128,1024]{1,0:T(8,128)} %copy.96), kind=kLoop, calls=%fused_computation.5 | loop fusion | flops 1572864 | bytes 4194304 | tf_op jit(solution)/shard_map/concatenate | solution.py:87
  36.5 2.2 fusion.109
  38.7 1.8 copy.168
  40.5 1.8 copy.167
  42.2 1.8 copy.166
  44.1 1.8 copy.165
  45.9 5.3 %all-gather.1 = f32[256,32]{0,1:T(8,128)S(1)} all-gather(f32[128,32]{0,1:T(8,128)S(1)} %pad_maximum_fusion.4), channel_id=3, replica_groups=mesh['text'=16,'video'=2] {'video'}, dimensions={0}, use_global_device_ids=true | all-gather | bytes 49152 | tf_op jit(solution)/shard_map/all_gather | solution.py:16
  51.2 2.6 %fusion.18 = (f32[128,8]{0,1:T(8,128)S(1)}, f32[128,8]{0,1:T(8,128)S(1)}, f32[128,8]{0,1:T(8,128)S(1)}, f32[128,8]{0,1:T(8,128)S(1)}) fusion(f32[128,8,256]{2,0,1:T(8,128)S(1)} %get-tuple-element.113, f32[128,8]{0,1:T(8,128)S(1)} %get-tuple-element.112, pred[128,256]{1,0:T(8,128)(4,1)S(1)} %compare_and_fusion, f32[128,8,256]{2,0,1:T(8,128)S(1)} %get-tuple-element.111, ...), kind=kLoop, calls=%fused_computation.52 | loop fusion | flops 3141632 | bytes 4259840 | tf_op jit(solution)/shard_map/reduce_sum | solution.py:76
  53.8 5.2 %all-gather.2 = f32[256,32]{0,1:T(8,128)S(1)} all-gather(f32[128,32]{0,1:T(8,128)S(1)} %pad_maximum_fusion.5), channel_id=4, replica_groups=mesh['text'=16,'video'=2] {'video'}, dimensions={0}, use_global_device_ids=true | all-gather | bytes 49152 | tf_op jit(solution)/shard_map/all_gather | solution.py:16
  59.1 0.4 convolution_bitcast_fusion
  59.5 0.4 convolution_bitcast_fusion.1
  59.9 0.4 convolution_bitcast_fusion.2
  60.4 0.4 convolution_bitcast_fusion.3
  60.8 0.8 pad_maximum_fusion.3
  61.6 2.0 copy.155
  64.0 0.7 copy.101
  64.7 0.7 copy.100
  65.4 31.1 %all-gather.5.cloned.1.call-done = f32[256,4096]{1,0:T(8,128)} async-done(((f32[128,4096]{1,0:T(8,128)}), f32[256,4096]{1,0:T(8,128)}) %all-gather.5.cloned.1.call-update) | async-done | bytes 4194320 | tf_op jit(solution)/shard_map/all_gather | solution.py:16
  96.6 0.6 broadcast_in_dim.113
  97.2 1.8 broadcast_in_dim.112
  99.0 0.6 broadcast_in_dim.111
  99.6 7.2 %multiply_bitcast_fusion = (f32[16,8,32,128]{3,1,2,0:T(8,128)S(1)}, bf16[128,4096]{1,0:T(8,128)(2,1)}) fusion(bf16[128,4096]{1,0:T(8,128)(2,1)S(1)} %copy-done.1, f32[16,8,32,128]{3,2,1,0:T(8,128)S(1)} %bitcast.159, f32[16,8,32,128]{3,2,1,0:T(8,128)S(1)} %bitcast.160, f32[256,4096]{1,0:T(8,128)S(1)} %copy-done.2, f32[16,8,32,128]{3,2,1,0:T(8,128)S(1)} %bitcast.161), kind=kLoop, calls=%fused_computation.7 | loop fusion | flops 4194304 | bytes 14680064
  106.8 1.7 copy.172
  108.5 2.2 reduce_sum.49
  110.8 0.8 fusion.111
  111.5 0.9 copy.121
  112.4 2.6 %fusion.13 = bf16[128,8,256]{2,0,1:T(8,128)(2,1)} fusion(bf16[128,8,128]{0,2,1:T(8,128)(2,1)} %bitcast.185, f32[128,8,256]{2,0,1:T(8,128)} %get-tuple-element.107, f32[128,8]{0,1:T(8,128)S(1)} %copy.121, f32[128,8]{0,1:T(8,128)S(1)} %copy-done.27, pred[128,256]{1,0:T(8,128)(4,1)S(1)} %compare_and_fusion, bf16[256,512]{1,0:T(8,128)(2,1)} %param.18), kind=kOutput, calls=%fused_computation.27 | convolution fusion | flops 68419584 | bytes 1941504 | tf_op jit(solution)/shard_map/rhd,cd->rhc/dot_general | solution.py:103
  115.0 0.9 copy.116
  116.0 2.2 fusion.12
  118.2 0.9 copy.111
  119.1 2.3 %fusion.11 = bf16[128,8,256]{2,0,1:T(8,128)(2,1)} fusion(bf16[128,8,128]{0,2,1:T(8,128)(2,1)} %bitcast.181, f32[128,8,256]{2,0,1:T(8,128)S(1)} %get-tuple-element.111, f32[128,8]{0,1:T(8,128)S(1)} %copy.111, f32[128,8]{0,1:T(8,128)S(1)} %copy-done.23, pred[128,256]{1,0:T(8,128)(4,1)S(1)} %compare_and_fusion, bf16[256,512]{1,0:T(8,128)(2,1)} %param.18), kind=kOutput, calls=%fused_computation.25 | convolution fusion | flops 68419584 | bytes 1941504 | tf_op jit(solution)/shard_map/rhd,cd->rhc/dot_general | solution.py:103
  121.4 1.5 fusion.10
  122.9 1.3 fusion.17
  124.2 1.3 fusion.16
  126.1 1.0 copy.153
  127.1 0.3 convolution_multiply_fusion.4
  127.4 0.3 convolution_multiply_fusion.5
  127.8 0.3 convolution_multiply_fusion.6
  128.7 0.3 convolution_multiply_fusion.7
  129.3 1.5 pad_maximum_fusion.1
  130.9 1.0 copy.156
  131.8 0.7 copy.128
  132.5 0.8 constant_dynamic-slice_fusion
  133.4 50.5 %reduce-scatter.10.cloned.1.call-done = f32[16,512]{1,0:T(8,128)} async-done(((f32[256,512]{1,0:T(8,128)}), f32[16,512]{1,0:T(8,128)}) %reduce-scatter.10.cloned.1.call-update) | async-done | bytes 32784
  183.9 0.9 copy.154
  184.7 0.7 copy.127
  185.4 31.3 %reduce-scatter.8.cloned.1.call-done = f32[128,2048]{1,0:T(8,128)} async-done(((f32[128,4096]{1,0:T(8,128)}), f32[128,2048]{1,0:T(8,128)}) %reduce-scatter.8.cloned.1.call-update) | async-done | bytes 1048592 | tf_op jit(solution)/shard_map/reduce_scatter | solution.py:126
  216.7 2.1 convert_element_type.65
  (87 shorter events, 2.6 us)
Async XLA Ops:
  8.0 1.6 copy-start.28
  8.0 3.7 %copy-start.29 = (s32[128]{0:T(128)S(1)}, s32[128]{0:T(128)}, u32[]{:S(2)}) copy-start(s32[128]{0:T(128)} %param.20) | copy-start | bytes 1540
  8.0 3.8 %copy-start.12 = (bf16[256,512]{1,0:T(8,128)(2,1)S(1)}, bf16[256,512]{1,0:T(8,128)(2,1)}, u32[]{:S(2)}) copy-start(bf16[256,512]{1,0:T(8,128)(2,1)} %param.17) | copy-start | bytes 786436
  8.0 88.5 %all-gather.5.cloned.1.call-start = ((), (), s32[]{:S(2)}) async-start(), calls=%async_computation.4 | async-start | bytes 6291456 | tf_op jit(solution)/shard_map/all_gather | solution.py:16
  10.3 3.4 %copy-start.4 = (bf16[128,1024]{0,1:T(8,128)(2,1)}, bf16[128,1024]{0,1:T(8,128)(2,1)S(1)}, u32[]{:S(2)}) copy-start(bf16[128,1024]{0,1:T(8,128)(2,1)S(1)} %copy.161) | copy-start | bytes 786436
  13.7 1.3 copy-start.6
  36.4 94.4 %reduce-scatter.12.cloned.1.call-start = ((), (), s32[]{:S(2)}) async-start(), calls=%async_computation.6 | async-start | bytes 557056
  51.2 7.9 %copy-start = (f32[128,8,256]{2,0,1:T(8,128)S(1)}, f32[128,8,256]{2,0,1:T(8,128)}, u32[]{:S(2)}) copy-start(f32[128,8,256]{2,0,1:T(8,128)} %get-tuple-element.107) | copy-start | bytes 3145732
  51.2 7.9 %copy-start.17 = (bf16[128,1024]{0,1:T(8,128)(2,1)S(1)}, bf16[128,1024]{0,1:T(8,128)(2,1)}, u32[]{:S(2)}) copy-start(bf16[128,1024]{0,1:T(8,128)(2,1)} %copy.168) | copy-start | bytes 786436
  51.2 8.3 %copy-start.16 = (bf16[128,1024]{0,1:T(8,128)(2,1)S(1)}, bf16[128,1024]{0,1:T(8,128)(2,1)}, u32[]{:S(2)}) copy-start(bf16[128,1024]{0,1:T(8,128)(2,1)} %copy.167) | copy-start | bytes 786436
  53.8 6.1 %copy-start.15 = (bf16[128,1024]{0,1:T(8,128)(2,1)S(1)}, bf16[128,1024]{0,1:T(8,128)(2,1)}, u32[]{:S(2)}) copy-start(bf16[128,1024]{0,1:T(8,128)(2,1)} %copy.166) | copy-start | bytes 786436
  59.0 1.3 copy-start.22
  59.0 1.3 copy-start.24
  59.1 1.3 copy-start.26
  59.1 1.3 copy-start.20
  59.1 1.2 copy-start.14
  63.7 120.2 %reduce-scatter.10.cloned.1.call-start = ((), (), s32[]{:S(2)}) async-start(), calls=%async_computation.5 | async-start | bytes 557056
  96.6 2.4 %copy-start.18 = (f32[128,32]{1,0:T(8,128)S(1)}, f32[128,32]{1,0:T(8,128)}, u32[]{:S(2)}) copy-start(f32[128,32]{1,0:T(8,128)} %copy.100) | copy-start | bytes 49156
  96.6 3.0 %copy-start.2 = (f32[256,4096]{1,0:T(8,128)S(1)}, f32[256,4096]{1,0:T(8,128)}, u32[]{:S(2)}) copy-start(f32[256,4096]{1,0:T(8,128)} %all-gather.5.cloned.1.call-done) | copy-start | bytes 12582916
  97.2 2.4 %copy-start.1 = (bf16[128,4096]{1,0:T(8,128)(2,1)S(1)}, bf16[128,4096]{1,0:T(8,128)(2,1)}, u32[]{:S(2)}) copy-start(bf16[128,4096]{1,0:T(8,128)(2,1)} %param.19) | copy-start | bytes 3145732
  108.5 3.9 %copy-start.27 = (f32[128,8]{0,1:T(8,128)S(1)}, f32[128,8]{0,1:T(8,128)}, u32[]{:S(2)}) copy-start(f32[128,8]{0,1:T(8,128)} %copy-done.26) | copy-start | bytes 12292
  108.5 7.5 %copy-start.25 = (f32[128,8]{0,1:T(8,128)S(1)}, f32[128,8]{0,1:T(8,128)}, u32[]{:S(2)}) copy-start(f32[128,8]{0,1:T(8,128)} %copy-done.24) | copy-start | bytes 12292
  111.5 7.5 %copy-start.23 = (f32[128,8]{0,1:T(8,128)S(1)}, f32[128,8]{0,1:T(8,128)}, u32[]{:S(2)}) copy-start(f32[128,8]{0,1:T(8,128)} %copy-done.22) | copy-start | bytes 12292
  115.0 6.3 %copy-start.19 = (f32[128,8]{1,0:T(8,128)S(1)}, f32[128,8]{1,0:T(8,128)}, u32[]{:S(2)}) copy-start(f32[128,8]{1,0:T(8,128)} %get-tuple-element.96) | copy-start | bytes 12292
  115.0 6.4 %copy-start.21 = (f32[128,8]{0,1:T(8,128)S(1)}, f32[128,8]{0,1:T(8,128)}, u32[]{:S(2)}) copy-start(f32[128,8]{0,1:T(8,128)} %copy-done.20) | copy-start | bytes 12292
  119.1 5.1 %copy-start.5 = (bf16[128,1024]{0,1:T(8,128)(2,1)S(1)}, bf16[128,1024]{0,1:T(8,128)(2,1)}, u32[]{:S(2)}) copy-start(bf16[128,1024]{0,1:T(8,128)(2,1)} %copy-done.4) | copy-start | bytes 786436
  121.4 4.1 %copy-start.7 = (bf16[128,1024]{0,1:T(8,128)(2,1)S(1)}, bf16[128,1024]{0,1:T(8,128)(2,1)}, u32[]{:S(2)}) copy-start(bf16[128,1024]{0,1:T(8,128)(2,1)} %copy-done.6) | copy-start | bytes 786436
  121.4 4.2 %copy-start.10 = (bf16[128,8,256]{2,0,1:T(8,128)(2,1)S(1)}, bf16[128,8,256]{2,0,1:T(8,128)(2,1)}, u32[]{:S(2)}) copy-start(bf16[128,8,256]{2,0,1:T(8,128)(2,1)} %fusion.11) | copy-start | bytes 1572868
  121.4 4.4 %copy-start.8 = (bf16[128,1024]{0,1:T(8,128)(2,1)S(1)}, bf16[128,1024]{0,1:T(8,128)(2,1)}, u32[]{:S(2)}) copy-start(bf16[128,1024]{0,1:T(8,128)(2,1)} %copy.157) | copy-start | bytes 786436
  125.5 1.6 copy-start.9
  125.5 1.6 copy-start.13
  125.8 1.6 copy-start.11
  127.8 89.0 %reduce-scatter.8.cloned.1.call-start = ((), (), s32[]{:S(2)}) async-start(), calls=%async_computation.3 | async-start | bytes 3145728 | tf_op jit(solution)/shard_map/reduce_scatter | solution.py:126
  130.8 1.7 copy-start.3
Sparse Core Ops, SparseCore 0:
  36.5 59.9 all-gather.4
Sparse Core Ops, SparseCore 1:
  63.7 57.6 reduce-scatter.11
  127.8 56.0 reduce-scatter.9
  186.0 30.7 reduce-scatter.7
where the time goes:
time: 228 us; the launch traced here: 226 us
  waiting for transfers between devices  113 us (50%)
  local copies, waits for them, and re-layouts  38.7 us (17%)
  matrix products  26.7 us (12%)
  other arithmetic  21.1 us (9%)
  between operations  16.2 us (7%)
  blocking collectives  10.5 us (5%)
    unnamed x6, waiting for transfers between devices  50.6 us
    reduce_scatter x1, waiting for transfers between devices, local(): lax.psum_scatter(query_terms, 'video', scatter_dimension=1, tiled=True)  31.3 us
    all_gather x1, waiting for transfers between devices, joined(): pieces = jax.tree.map(lambda part: lax.all_gather(part, axis), value)  31.1 us
    unnamed x75, local copies, waits for them, and re-layouts  16.7 us
    all_gather x2, blocking collectives, joined(): pieces = jax.tree.map(lambda part: lax.all_gather(part, axis), value)  10.5 us
    dot_general x4, matrix products, local(): jnp.einsum('rhc,cd->rhd', weights.astype(jnp.bfloat16), value_grp, prefer...  8.66 us
    dot_general x4, matrix products, local(): jnp.einsum('rhd,cd->rhc', grad_grp, value_grp, preferred_element_type=jnp...  8.61 us
    reshape x4, local copies, waits for them, and re-layouts, local(): partial_value.append(jnp.einsum('rhc,cd->rhd', weights.astype(jnp.bfloat1...  8.19 us
  transfers between devices with their start and end apart: 4, of which 3 were waited for; matrix products, arithmetic and copies ran while one was open for 25% of the time, Pallas kernels for 0%

commit v1 on v0

v1 whole, which is shorter than its diff:
```python
import functools
import math

import jax
import jax.numpy as jnp
from jax import lax
from jax.experimental import pallas as pl
from jax.experimental.pallas import tpu as pltpu
from jax.sharding import PartitionSpec as P

H = 32
G = 4
HD = 128
PER_GROUP = H // G
CORES = 2
DEPTH = 4
FLOOR = -1e30
MESH = pl.DeviceIdType.MESH
NT = (((1,), (1,)), ((), ()))


def remote(src, dst, send, recv, text, video):
    return pltpu.make_async_remote_copy(
        src_ref=src,
        dst_ref=dst,
        send_sem=send,
        recv_sem=recv,
        device_id=(text, video),
        device_id_type=MESH,
    )


def kernel(
    T, V, q_ref, go_ref, k_ref, v_ref, pos_ref, span_ref,
    att_ref, dq_ref, dk_ref, dv_ref,
    q_s, go_s, kv_s, kv_out, kv_in, k_all, v_all, bias, p_all, ds_all,
    part, r_core, s_y, r_y, s_z, r_z, s_x, r_x, att_s, dq_s,
    load_sem, out_sem, kv_send, kv_recv, fw_send, fw_recv,
    c_send, c_recv, y_send, y_recv, z_send, z_recv, x_send, x_recv,
):
    Z = DEPTH
    Y = T // (CORES * Z)
    heads = H // V
    groups = max(1, heads // PER_GROUP)
    gheads = heads // groups
    own = kv_s.shape[1]
    half = own // CORES
    gw = groups * HD
    tokens = own * V
    R = own // T
    scale = HD ** -0.5

    t = lax.axis_index("text")
    v = lax.axis_index("video")
    c = lax.rem(t, CORES)
    y = lax.rem(t // CORES, Y)
    z = t // (CORES * Y)
    sib = t + 1 - 2 * c

    def text_at(zz, yy):
        return (zz * Y + yy) * CORES + c

    def key_column(rank):
        return pl.multiple_of(((rank * heads) // PER_GROUP) * HD, HD)

    loads = [
        pltpu.make_async_copy(k_ref, kv_s.at[0], load_sem.at[0]),
        pltpu.make_async_copy(v_ref, kv_s.at[1], load_sem.at[1]),
    ]
    for gi in range(groups):
        cols = pl.ds(pl.multiple_of((v * heads + gi * gheads) * HD, HD), gheads * HD)
        loads.append(pltpu.make_async_copy(q_ref.at[:, cols], q_s.at[gi], load_sem.at[2 + 2 * gi]))
        loads.append(pltpu.make_async_copy(go_ref.at[:, cols], go_s.at[gi], load_sem.at[3 + 2 * gi]))
    for load in loads:
        load.start()

    barrier = pltpu.get_barrier_semaphore()
    partners = [(sib, v)]
    partners += [(t, lax.rem(v + k, V)) for k in range(1, V)]
    partners += [(text_at(z, lax.rem(y + k, Y)), v) for k in range(1, Y)]
    partners += [(text_at(lax.rem(z + k, Z), y), v) for k in range(1, Z)]
    for partner in partners:
        pl.semaphore_signal(barrier, inc=1, device_id=partner, device_id_type=MESH)

    loads[0].wait()
    loads[1].wait()
    rows = pl.ds(pl.multiple_of(c * half, half), half)
    for k in range(1, V):
        cols = pl.ds(key_column(lax.rem(v + k, V)), gw)
        for i in range(2):
            kv_out[k - 1, i] = kv_s[i, rows, cols].astype(jnp.float32)
    pl.semaphore_wait(barrier, len(partners))
    sends = []
    for k in range(1, V):
        copy = remote(kv_out.at[k - 1], kv_in.at[v, c], kv_send.at[k - 1], kv_recv.at[k - 1], t, lax.rem(v + k, V))
        copy.start()
        sends.append(copy)

    pos = pos_ref[...]
    low = span_ref[0, 0]
    high = span_ref[0, 1]
    token = lax.broadcasted_iota(jnp.int32, (tokens, HD), 0)
    bias[...] = jnp.where((token >= low) & (token < high) & (token <= pos), 0.0, FLOOR)
    mine = pl.ds(pl.multiple_of(v * own, own), own)
    cols = pl.ds(key_column(v), gw)
    k_all[mine, :] = kv_s[0, :, cols].astype(jnp.float32)
    v_all[mine, :] = kv_s[1, :, cols].astype(jnp.float32)

    forwards = []
    for k in range(1, V):
        source = lax.rem(v - k + V, V)
        sends[k - 1].wait_recv()
        copy = remote(kv_in.at[source, c], kv_in.at[source, c], fw_send.at[k - 1], fw_recv.at[k - 1], sib, v)
        copy.start()
        forwards.append(copy)
        there = pl.ds(pl.multiple_of(source * own + c * half, half), half)
        k_all[there, :] = kv_in[source, c, 0]
        v_all[there, :] = kv_in[source, c, 1]
    for k in range(1, V):
        source = lax.rem(v - k + V, V)
        forwards[k - 1].wait_recv()
        there = pl.ds(pl.multiple_of(source * own + (1 - c) * half, half), half)
        k_all[there, :] = kv_in[source, 1 - c, 0]
        v_all[there, :] = kv_in[source, 1 - c, 1]
    for load in loads[2:]:
        load.wait()

    pending = list(sends) + list(forwards)
    running = {}

    def start_core(gi):
        copy = remote(part.at[gi, 1 - c], r_core.at[gi], c_send.at[gi], c_recv.at[gi], sib, v)
        copy.start()
        running[gi] = [copy]

    def start_y(gi):
        running[gi][0].wait_recv()
        pending.extend(running[gi])
        s_y[gi] = part[gi, c] + r_core[gi]
        running[gi] = []
        for k in range(1, Y):
            yy = lax.rem(y + k, Y)
            copy = remote(s_y.at[gi, yy], r_y.at[gi, k - 1], y_send.at[gi, k - 1], y_recv.at[gi, k - 1], text_at(z, yy), v)
            copy.start()
            running[gi].append(copy)

    def start_z(gi):
        total = s_y[gi, y]
        for k in range(1, Y):
            running[gi][k - 1].wait_recv()
            total += r_y[gi, k - 1]
        pending.extend(running[gi])
        s_z[gi] = total
        running[gi] = []
        for k in range(1, Z):
            zz = lax.rem(z + k, Z)
            copy = remote(s_z.at[gi, zz], r_z.at[gi, k - 1], z_send.at[gi, k - 1], z_recv.at[gi, k - 1], text_at(zz, y), v)
            copy.start()
            running[gi].append(copy)

    def start_x(gi):
        total = s_z[gi, z]
        for k in range(1, Z):
            running[gi][k - 1].wait_recv()
            total += r_z[gi, k - 1]
        pending.extend(running[gi])
        s_x[gi] = total
        running[gi] = []
        for k in range(1, V):
            vv = lax.rem(v + k, V)
            copy = remote(s_x.at[gi, vv], r_x.at[gi, v], x_send.at[gi, k - 1], x_recv.at[gi, k - 1], t, vv)
            copy.start()
            running[gi].append(copy)
        r_x[gi, v] = s_x[gi, v]

    outs = []
    bias_pair = jnp.concatenate([bias[...]] * 2, axis=1)
    for gi in range(groups):
        kf = k_all[:, gi * HD : (gi + 1) * HD]
        vf = v_all[:, gi * HD : (gi + 1) * HD]
        kb = kf.astype(jnp.bfloat16)
        vb = vf.astype(jnp.bfloat16)
        kt = kf.T.astype(jnp.bfloat16)
        vt = vf.T.astype(jnp.bfloat16)
        for pair in range(gheads // 2):
            heads_here = (2 * pair, 2 * pair + 1)
            qp = jnp.concatenate([q_s[gi, :, h * HD : (h + 1) * HD] for h in heads_here], axis=0)
            gp = jnp.concatenate([go_s[gi, :, h * HD : (h + 1) * HD] for h in heads_here], axis=0)
            s = lax.dot_general(kb, qp, NT, preferred_element_type=jnp.float32)
            s = s * (scale * math.log2(math.e)) + bias_pair
            e = jnp.exp2(s - jnp.max(s, axis=0, keepdims=True))
            prob = e * (1.0 / jnp.sum(e, axis=0, keepdims=True))
            low_prob = prob.astype(jnp.bfloat16)
            dprob = lax.dot_general(vb, gp, NT, preferred_element_type=jnp.float32)
            delta = jnp.sum(prob * dprob, axis=0, keepdims=True)
            dscore = (prob * (dprob - delta)).astype(jnp.bfloat16)
            there = slice(pair * 2 * HD, (pair + 1) * 2 * HD)
            p_all[gi, :, there] = low_prob
            ds_all[gi, :, there] = dscore
            out = jnp.dot(vt, low_prob, preferred_element_type=jnp.float32).T.astype(jnp.bfloat16)
            dq = (jnp.dot(kt, dscore, preferred_element_type=jnp.float32) * scale).T.astype(jnp.bfloat16)
            for i, h in enumerate(heads_here):
                att_s[gi, :, h * HD : (h + 1) * HD] = out[i * HD : (i + 1) * HD]
                dq_s[gi, :, h * HD : (h + 1) * HD] = dq[i * HD : (i + 1) * HD]
            if gi > 0 and pair == 0:
                start_y(gi - 1)
            if gi > 0 and pair == gheads // 2 - 1:
                start_z(gi - 1)
        cols = slice(gi * gheads * HD, (gi + 1) * gheads * HD)
        for i, (src, dst) in enumerate(((att_s, att_ref), (dq_s, dq_ref))):
            copy = pltpu.make_async_copy(src.at[gi], dst.at[:, cols], out_sem.at[gi, i])
            copy.start()
            outs.append(copy)
        qg = jnp.concatenate([q_s[gi, :, h * HD : (h + 1) * HD] for h in range(gheads)], axis=0)
        gg = jnp.concatenate([go_s[gi, :, h * HD : (h + 1) * HD] for h in range(gheads)], axis=0)
        dk = jnp.dot(ds_all[gi], qg, preferred_element_type=jnp.float32) * scale
        dv = jnp.dot(p_all[gi], gg, preferred_element_type=jnp.float32)
        for i, grad in enumerate((dk, dv)):
            for vv in range(V):
                for zz in range(Z):
                    for yy in range(Y):
                        for cc in range(CORES):
                            at = (((vv * Z + zz) * Y + yy) * CORES + cc) * R
                            part[gi, cc, yy, zz, vv, i] = grad[at : at + R]
        start_core(gi)

    last = groups - 1
    if groups > 1:
        start_y(last)
        for gi in range(groups - 1):
            start_x(gi)
        start_z(last)
        start_x(last)
    else:
        start_y(last)
        start_z(last)
        start_x(last)
    for gi in range(groups):
        for copy in running[gi]:
            copy.wait_recv()
        pending.extend(running[gi])
    for g in range(G):
        if V <= G:
            found = [(g % groups, g // groups)]
        else:
            share = V // G
            found = [(0, g * share + i) for i in range(share)]
        total = sum(r_x[gi, rank] for gi, rank in found)
        dk_ref[:, g * HD : (g + 1) * HD] = total[0].astype(jnp.bfloat16)
        dv_ref[:, g * HD : (g + 1) * HD] = total[1].astype(jnp.bfloat16)
    for copy in pending:
        copy.wait_send()
    for copy in outs:
        copy.wait()


def local(T, V, queries, video_keys, video_values, grad_out, positions, span_bounds):
    Z = DEPTH
    Y = T // (CORES * Z)
    rows = queries.shape[0]
    own = video_keys.shape[0]
    tokens = own * V
    heads = H // V
    groups = max(1, heads // PER_GROUP)
    gheads = heads // groups
    gw = groups * HD
    R = own // T
    f32, bf16 = jnp.float32, jnp.bfloat16
    dma = pltpu.SemaphoreType.DMA
    hbm = pl.BlockSpec(memory_space=pl.ANY)
    vmem = pl.BlockSpec(memory_space=pltpu.VMEM)
    smem = pl.BlockSpec(memory_space=pltpu.SMEM)
    scratch = [
        pltpu.VMEM((groups, rows, gheads * HD), bf16),
        pltpu.VMEM((groups, rows, gheads * HD), bf16),
        pltpu.VMEM((2, own, G * HD), bf16),
        pltpu.VMEM((V - 1, 2, own // CORES, gw), f32),
        pltpu.VMEM((V, CORES, 2, own // CORES, gw), f32),
        pltpu.VMEM((tokens, gw), f32),
        pltpu.VMEM((tokens, gw), f32),
        pltpu.VMEM((tokens, rows), f32),
        pltpu.VMEM((groups, tokens, gheads * rows), bf16),
        pltpu.VMEM((groups, tokens, gheads * rows), bf16),
        pltpu.VMEM((groups, CORES, Y, Z, V, 2, R, HD), f32),
        pltpu.VMEM((groups, Y, Z, V, 2, R, HD), f32),
        pltpu.VMEM((groups, Y, Z, V, 2, R, HD), f32),
        pltpu.VMEM((groups, Y - 1, Z, V, 2, R, HD), f32),
        pltpu.VMEM((groups, Z, V, 2, R, HD), f32),
        pltpu.VMEM((groups, Z - 1, V, 2, R, HD), f32),
        pltpu.VMEM((groups, V, 2, R, HD), f32),
        pltpu.VMEM((groups, V, 2, R, HD), f32),
        pltpu.VMEM((groups, rows, gheads * HD), bf16),
        pltpu.VMEM((groups, rows, gheads * HD), bf16),
        dma((2 + 2 * groups,)),
        dma((groups, 2)),
        dma((V - 1,)), dma((V - 1,)), dma((V - 1,)), dma((V - 1,)),
        dma((groups,)), dma((groups,)),
        dma((groups, Y - 1)), dma((groups, Y - 1)),
        dma((groups, Z - 1)), dma((groups, Z - 1)),
        dma((groups, V - 1)), dma((groups, V - 1)),
    ]
    return pl.pallas_call(
        functools.partial(kernel, T, V),
        out_shape=(
            jax.ShapeDtypeStruct((rows, heads * HD), bf16),
            jax.ShapeDtypeStruct((rows, heads * HD), bf16),
            jax.ShapeDtypeStruct((R, G * HD), bf16),
            jax.ShapeDtypeStruct((R, G * HD), bf16),
        ),
        in_specs=[hbm, hbm, hbm, hbm, vmem, smem],
        out_specs=(hbm, hbm, vmem, vmem),
        scratch_shapes=scratch,
        compiler_params=pltpu.CompilerParams(
            collective_id=0, has_side_effects=True, vmem_limit_bytes=56 * 1024 * 1024
        ),
        cost_estimate=pl.CostEstimate(
            flops=12 * rows * heads * tokens * HD,
            bytes_accessed=8 * rows * heads * HD + 4 * own * G * HD,
            transcendentals=rows * heads * tokens,
        ),
        name="attention",
    )(queries, grad_out, video_keys, video_values, positions.reshape(1, rows), span_bounds)


def solution(mesh):
    placed = (
        P("text", None),
        P("video", None),
        P("video", None),
        P("text", None),
        P("text"),
        P("text", None),
    )
    return jax.shard_map(
        functools.partial(local, mesh.shape["text"], mesh.shape["video"]),
        mesh=mesh,
        in_specs=placed,
        out_specs=(
            P("text", "video"),
            P("text", "video"),
            P(("video", "text"), None),
            P(("video", "text"), None),
        ),
        check_vma=False,
    )
```

time: 228 us -> 41.6 us (0.18)
  waiting for transfers between devices: 113 us -> 0 us
  Pallas kernels: 0 us -> 36.6 us
  local copies, waits for them, and re-layouts: 38.7 us -> 4.07 us
  matrix products: 26.7 us -> 0 us
  other arithmetic: 21.1 us -> 0 us
  between operations: 16.2 us -> 0.65 us
  blocking collectives: 10.5 us -> 0 us
    unnamed x6 -> x0, waiting for transfers between devices: 50.6 us -> none
    pallas_call x0 -> x1, Pallas kernels: none -> 36.6 us  [local(): pl.pallas_call(functools.partial(kernel, T, V), out_shape=(jax.ShapeDtype...]
    reduce_scatter x1 -> x0, waiting for transfers between devices: 31.3 us -> none  [local(): lax.psum_scatter(query_terms, 'video', scatter_dimension=1, tiled=True)]
    all_gather x1 -> x0, waiting for transfers between devices: 31.1 us -> none  [joined(): pieces = jax.tree.map(lambda part: lax.all_gather(part, axis), value)]
    dot_general x24 -> x0, matrix products: 26.7 us -> none  [the longest x4 8.66 us: local(): jnp.einsum('rhc,cd->rhd', weights.astype(jnp.bfloat16), value_grp, prefer...]
    unnamed x75 -> x10, local copies, waits for them, and re-layouts: 16.7 us -> 4.07 us
    all_gather x2 -> x0, blocking collectives: 10.5 us -> none  [joined(): pieces = jax.tree.map(lambda part: lax.all_gather(part, axis), value)]
    reshape x4 -> x0, local copies, waits for them, and re-layouts: 8.19 us -> none  [local(): partial_value.append(jnp.einsum('rhc,cd->rhd', weights.astype(jnp.bfloat1...]
  transfers between devices with their start and end apart: 4 -> 0, of which waited for: 3 -> 0; matrix products, arithmetic and copies ran while one was open for 25% -> 0% of each run, Pallas kernels for 0% -> 0%
where the time goes in v1:
time: 41.6 us; the launch traced here: 41.3 us
  Pallas kernels  36.6 us (88%)
  local copies, waits for them, and re-layouts  4.07 us (10%)
  between operations  0.65 us (2%)
    pallas_call x1, Pallas kernels, local(): pl.pallas_call(functools.partial(kernel, T, V), out_shape=(jax.ShapeDtype...  36.6 us
    unnamed x10, local copies, waits for them, and re-layouts  4.07 us

profile of v1, /device:TPU:0, one launch (start us, length us, event | category | flops | bytes accessed | tf_op | source)
XLA Modules:
  0.0 41.3 jit_solution(13231693456690113872)
XLA Ops:
  0.6 36.6 %attention.1 = (bf16[128,2048]{1,0:T(8,128)(2,1)}, bf16[128,2048]{1,0:T(8,128)(2,1)}, bf16[16,512]{1,0:T(8,128)(2,1)}, bf16[16,512]{1,0:T(8,128)(2,1)}) custom-call(bf16[128,4096]{1,0:T(8,128)(2,1)} %q_ref.1, bf16[128,4096]{1,0:T(8,128)(2,1)} %go_ref.1, bf16[256,512]{1,0:T(8,128)(2,1)} %k_ref.1, bf16[256,512]{1,0:T(8,128)(2,1)} %v_ref.1, s32[1,128]{1,0:T(1,128)} %bitcast.1, ...), custom_call_target="tpu_custom_call" | custom-call | flops 1610612736 | bytes 2621440 | tf_op jit(solution)/shard_map/attention/pallas_call | solution.py:302
  37.2 0.0 copy-start
  37.2 1.9 %copy.14 = bf16[128,2048]{1,0:T(8,128)(2,1)} copy(bf16[128,2048]{1,0:T(8,128)(2,1)} %get-tuple-element.8) | data formatting | bytes 1048576
  39.2 0.0 copy-done
  39.2 0.0 copy-start.2
  39.2 0.8 %copy.15 = bf16[128,2048]{1,0:T(8,128)(2,1)} copy(bf16[128,2048]{1,0:T(8,128)(2,1)S(1)} %copy-done) | data formatting | bytes 1048576
  40.0 0.0 copy-done.2
  40.0 0.0 copy-start.1
  40.0 0.6 %copy.16 = bf16[16,512]{1,0:T(8,128)(2,1)} copy(bf16[16,512]{1,0:T(8,128)(2,1)S(1)} %copy-done.2) | data formatting | bytes 32768
  40.6 0.1 copy-done.1
  40.7 0.6 %copy.17 = bf16[16,512]{1,0:T(8,128)(2,1)} copy(bf16[16,512]{1,0:T(8,128)(2,1)S(1)} %copy-done.1) | data formatting | bytes 32768
Async XLA Ops:
  37.2 2.0 %copy-start = (bf16[128,2048]{1,0:T(8,128)(2,1)S(1)}, bf16[128,2048]{1,0:T(8,128)(2,1)}, u32[]{:S(2)}) copy-start(bf16[128,2048]{1,0:T(8,128)(2,1)} %get-tuple-element.9) | copy-start | bytes 1572868
  39.2 0.8 %copy-start.2 = (bf16[16,512]{1,0:T(8,128)(2,1)S(1)}, bf16[16,512]{1,0:T(8,128)(2,1)}, u32[]{:S(2)}) copy-start(bf16[16,512]{1,0:T(8,128)(2,1)} %get-tuple-element.10) | copy-start | bytes 49156
  40.0 0.7 %copy-start.1 = (bf16[16,512]{1,0:T(8,128)(2,1)S(1)}, bf16[16,512]{1,0:T(8,128)(2,1)}, u32[]{:S(2)}) copy-start(bf16[16,512]{1,0:T(8,128)(2,1)} %get-tuple-element.11) | copy-start | bytes 49156

commit v2 on v1

v2 whole, which is shorter than its diff:
```python
import functools
import math

import jax
import jax.numpy as jnp
from jax import lax
from jax.experimental import pallas as pl
from jax.experimental.pallas import tpu as pltpu
from jax.sharding import PartitionSpec as P

H = 32
G = 4
HD = 128
PER_GROUP = H // G
CORES = 2
DEPTH = 4
FLOOR = -1e30
MESH = pl.DeviceIdType.MESH
NT = (((1,), (1,)), ((), ()))


def remote(src, dst, send, recv, text, video):
    return pltpu.make_async_remote_copy(
        src_ref=src,
        dst_ref=dst,
        send_sem=send,
        recv_sem=recv,
        device_id=(text, video),
        device_id_type=MESH,
    )


def kernel(
    T, V, q_ref, go_ref, k_ref, v_ref, pos_ref, span_ref,
    att_ref, dq_ref, dk_ref, dv_ref,
    q_s, go_s, kv_s, kv_out, kv_in, kv_all, bias, s_all, dp_own, p_all, ds_all,
    part, r_core, s_y, r_y, s_z, r_z, s_x, r_x, att_s, dq_s,
    load_sem, out_sem, kv_send, kv_recv, fw_send, fw_recv,
    c_send, c_recv, y_send, y_recv, z_send, z_recv, x_send, x_recv,
):
    Z = DEPTH
    Y = T // (CORES * Z)
    heads = H // V
    groups = max(1, heads // PER_GROUP)
    gheads = heads // groups
    own = kv_s.shape[1]
    half = own // CORES
    gw = groups * HD
    R = own // T
    scale = HD ** -0.5
    f32, bf16 = jnp.float32, jnp.bfloat16

    t = lax.axis_index("text")
    v = lax.axis_index("video")
    c = lax.rem(t, CORES)
    y = lax.rem(t // CORES, Y)
    z = t // (CORES * Y)
    sib = t + 1 - 2 * c

    def text_at(zz, yy):
        return (zz * Y + yy) * CORES + c

    def key_column(rank):
        return pl.multiple_of(((rank * heads) // PER_GROUP) * HD, HD)

    def source(k):
        return lax.rem(v - k + V, V)

    loads = [
        pltpu.make_async_copy(k_ref, kv_s.at[0], load_sem.at[0]),
        pltpu.make_async_copy(v_ref, kv_s.at[1], load_sem.at[1]),
    ]
    for gi in range(groups):
        cols = pl.ds(pl.multiple_of((v * heads + gi * gheads) * HD, HD), gheads * HD)
        loads.append(pltpu.make_async_copy(q_ref.at[:, cols], q_s.at[gi], load_sem.at[2 + 2 * gi]))
        loads.append(pltpu.make_async_copy(go_ref.at[:, cols], go_s.at[gi], load_sem.at[3 + 2 * gi]))
    for load in loads:
        load.start()

    barrier = pltpu.get_barrier_semaphore()
    partners = [(sib, v)]
    partners += [(t, lax.rem(v + k, V)) for k in range(1, V)]
    partners += [(text_at(z, lax.rem(y + k, Y)), v) for k in range(1, Y)]
    partners += [(text_at(lax.rem(z + k, Z), y), v) for k in range(1, Z)]
    for partner in partners:
        pl.semaphore_signal(barrier, inc=1, device_id=partner, device_id_type=MESH)

    loads[0].wait()
    loads[1].wait()
    rows = pl.ds(pl.multiple_of(c * half, half), half)
    rest = pl.ds(pl.multiple_of((1 - c) * half, half), half)
    for k in range(1, V):
        cols = pl.ds(key_column(lax.rem(v + k, V)), gw)
        for i in range(2):
            kv_out[i, k - 1] = kv_s[i, rows, cols].astype(f32)
    pl.semaphore_wait(barrier, len(partners))
    sends = [[], []]
    for i in range(2):
        for k in range(1, V):
            copy = remote(
                kv_out.at[i, k - 1], kv_in.at[i, k - 1, c], kv_send.at[i, k - 1], kv_recv.at[i, k - 1], t, lax.rem(v + k, V)
            )
            copy.start()
            sends[i].append(copy)
    forwards = [[], []]

    def forward(i):
        for k in range(1, V):
            sends[i][k - 1].wait_recv()
            copy = remote(
                kv_in.at[i, k - 1, c], kv_in.at[i, k - 1, c], fw_send.at[i, k - 1], fw_recv.at[i, k - 1], sib, v
            )
            copy.start()
            forwards[i].append(copy)
            kv_all[i, k, rows, :] = kv_in[i, k - 1, c]

    def collect(i):
        for k in range(1, V):
            forwards[i][k - 1].wait_recv()
            kv_all[i, k, rest, :] = kv_in[i, k - 1, 1 - c]

    pending = []
    flying = []

    def start_core(p):
        copy = remote(part.at[p, 1 - c], r_core.at[p], c_send.at[p], c_recv.at[p], sib, v)
        copy.start()
        return [copy]

    def start_y(p, before):
        before[0].wait_recv()
        s_y[p] = part[p, c] + r_core[p]
        copies = []
        for k in range(1, Y):
            yy = lax.rem(y + k, Y)
            copy = remote(s_y.at[p, yy], r_y.at[p, k - 1], y_send.at[p, k - 1], y_recv.at[p, k - 1], text_at(z, yy), v)
            copy.start()
            copies.append(copy)
        return copies

    def start_z(p, before):
        total = s_y[p, y]
        for k in range(1, Y):
            before[k - 1].wait_recv()
            total += r_y[p, k - 1]
        s_z[p] = total
        copies = []
        for k in range(1, Z):
            zz = lax.rem(z + k, Z)
            copy = remote(s_z.at[p, zz], r_z.at[p, k - 1], z_send.at[p, k - 1], z_recv.at[p, k - 1], text_at(zz, y), v)
            copy.start()
            copies.append(copy)
        return copies

    def start_x(p, before):
        total = s_z[p, z]
        for k in range(1, Z):
            before[k - 1].wait_recv()
            total += r_z[p, k - 1]
        s_x[p] = total
        copies = []
        for k in range(1, V):
            vv = lax.rem(v + k, V)
            copy = remote(s_x.at[p, vv], r_x.at[p, v], x_send.at[p, k - 1], x_recv.at[p, k - 1], t, vv)
            copy.start()
            copies.append(copy)
        r_x[p, v] = s_x[p, v]
        return copies

    stages = (start_y, start_z, start_x)

    def launch(p, grad):
        for j in range(V):
            for zz in range(Z):
                for yy in range(Y):
                    for cc in range(CORES):
                        at = j * own + ((zz * Y + yy) * CORES + cc) * R
                        part[p, cc, yy, zz, source(j)] = grad[at : at + R]
        flying.append([p, 0, start_core(p)])

    def tick():
        for piece in reversed(flying):
            p, stage, copies = piece
            if stage < len(stages):
                pending.extend(copies)
                piece[2] = stages[stage](p, copies)
                piece[1] = stage + 1

    pos = pos_ref[...]
    low = span_ref[0, 0]
    high = span_ref[0, 1]
    for j in range(V):
        token = source(j) * own + lax.broadcasted_iota(jnp.int32, (own, HD), 0)
        bias[j] = jnp.where((token >= low) & (token < high) & (token <= pos), 0.0, FLOOR)
    cols = pl.ds(key_column(v), gw)
    for i in range(2):
        kv_all[i, 0] = kv_s[i, :, cols].astype(f32)
    for load in loads[2:]:
        load.wait()

    pairs = gheads // 2

    def head_rows(ref, gi, first, count):
        return jnp.concatenate([ref[gi, :, h * HD : (h + 1) * HD] for h in range(first, first + count)], axis=0)

    def key_rows(i, gi, j):
        return kv_all[i, j, :, gi * HD : (gi + 1) * HD].astype(bf16)

    def scores(keys, queries, j):
        raw = lax.dot_general(keys, queries, NT, preferred_element_type=f32)
        return raw * (scale * math.log2(math.e)) + jnp.concatenate([bias[j]] * 2, axis=1)

    for gi in range(groups):
        keys = key_rows(0, gi, 0)
        values = key_rows(1, gi, 0)
        for pair in range(pairs):
            there = slice(pair * 2 * HD, (pair + 1) * 2 * HD)
            s_all[gi, 0, :, there] = scores(keys, head_rows(q_s, gi, 2 * pair, 2), 0)
            dp_own[gi, :, there] = lax.dot_general(
                values, head_rows(go_s, gi, 2 * pair, 2), NT, preferred_element_type=f32
            )

    forward(0)
    collect(0)
    for gi in range(groups):
        keys = [key_rows(0, gi, j) for j in range(V)]
        for pair in range(pairs):
            there = slice(pair * 2 * HD, (pair + 1) * 2 * HD)
            queries = head_rows(q_s, gi, 2 * pair, 2)
            s = [s_all[gi, 0, :, there]] + [scores(keys[j], queries, j) for j in range(1, V)]
            peak = functools.reduce(jnp.maximum, [jnp.max(x, axis=0, keepdims=True) for x in s])
            e = [jnp.exp2(x - peak) for x in s]
            inverse = 1.0 / sum(jnp.sum(x, axis=0, keepdims=True) for x in e)
            for j in range(V):
                prob = e[j] * inverse
                s_all[gi, j, :, there] = prob
                p_all[gi, j * own : (j + 1) * own, there] = prob.astype(bf16)
            if gi > 0 and pair == pairs // 2 - 1:
                tick()
        grad = jnp.dot(p_all[gi], head_rows(go_s, gi, 0, gheads), preferred_element_type=f32)
        launch(gi, grad)
        if gi == 0:
            forward(1)

    collect(1)
    outs = []
    for gi in range(groups):
        kt = jnp.concatenate([kv_all[0, j, :, gi * HD : (gi + 1) * HD].T for j in range(V)], axis=1).astype(bf16)
        vt = jnp.concatenate([kv_all[1, j, :, gi * HD : (gi + 1) * HD].T for j in range(V)], axis=1).astype(bf16)
        values = [key_rows(1, gi, j) for j in range(V)]
        for pair in range(pairs):
            there = slice(pair * 2 * HD, (pair + 1) * 2 * HD)
            gp = head_rows(go_s, gi, 2 * pair, 2)
            dprob = [dp_own[gi, :, there]] + [
                lax.dot_general(values[j], gp, NT, preferred_element_type=f32) for j in range(1, V)
            ]
            prob = [s_all[gi, j, :, there] for j in range(V)]
            delta = sum(jnp.sum(prob[j] * dprob[j], axis=0, keepdims=True) for j in range(V))
            for j in range(V):
                ds_all[gi, j * own : (j + 1) * own, there] = (prob[j] * (dprob[j] - delta)).astype(bf16)
            out = jnp.dot(vt, p_all[gi, :, there], preferred_element_type=f32).T.astype(bf16)
            dq = (jnp.dot(kt, ds_all[gi, :, there], preferred_element_type=f32) * scale).T.astype(bf16)
            for i in range(2):
                h = 2 * pair + i
                att_s[gi, :, h * HD : (h + 1) * HD] = out[i * HD : (i + 1) * HD]
                dq_s[gi, :, h * HD : (h + 1) * HD] = dq[i * HD : (i + 1) * HD]
            if pair == pairs // 2 - 1:
                tick()
        grad = jnp.dot(ds_all[gi], head_rows(q_s, gi, 0, gheads), preferred_element_type=f32) * scale
        launch(groups + gi, grad)
        cols = slice(gi * gheads * HD, (gi + 1) * gheads * HD)
        for i, (src, dst) in enumerate(((att_s, att_ref), (dq_s, dq_ref))):
            copy = pltpu.make_async_copy(src.at[gi], dst.at[:, cols], out_sem.at[gi, i])
            copy.start()
            outs.append(copy)

    for _ in stages:
        tick()
    for _, _, copies in flying:
        for copy in copies:
            copy.wait_recv()
        pending.extend(copies)
    for g in range(G):
        if V <= G:
            found = [(g % groups, g // groups)]
        else:
            share = V // G
            found = [(0, g * share + i) for i in range(share)]
        there = slice(g * HD, (g + 1) * HD)
        dv_ref[:, there] = sum(r_x[gi, rank] for gi, rank in found).astype(bf16)
        dk_ref[:, there] = sum(r_x[groups + gi, rank] for gi, rank in found).astype(bf16)
    for copy in pending + sends[0] + sends[1] + forwards[0] + forwards[1]:
        copy.wait_send()
    for copy in outs:
        copy.wait()


def hand_on(*refs):
    count = (len(refs) - 1) // 2
    sems = refs[-1]
    copies = [pltpu.make_async_copy(refs[i], refs[count + i], sems.at[i]) for i in range(count)]
    for copy in copies:
        copy.start()
    for copy in copies:
        copy.wait()


def local(T, V, queries, video_keys, video_values, grad_out, positions, span_bounds):
    Z = DEPTH
    Y = T // (CORES * Z)
    rows = queries.shape[0]
    own = video_keys.shape[0]
    tokens = own * V
    heads = H // V
    groups = max(1, heads // PER_GROUP)
    gheads = heads // groups
    gw = groups * HD
    R = own // T
    f32, bf16 = jnp.float32, jnp.bfloat16
    dma = pltpu.SemaphoreType.DMA
    hbm = pl.BlockSpec(memory_space=pl.ANY)
    vmem = pl.BlockSpec(memory_space=pltpu.VMEM)
    smem = pl.BlockSpec(memory_space=pltpu.SMEM)
    pieces = 2 * groups
    scratch = [
        pltpu.VMEM((groups, rows, gheads * HD), bf16),
        pltpu.VMEM((groups, rows, gheads * HD), bf16),
        pltpu.VMEM((2, own, G * HD), bf16),
        pltpu.VMEM((2, V - 1, own // CORES, gw), f32),
        pltpu.VMEM((2, V - 1, CORES, own // CORES, gw), f32),
        pltpu.VMEM((2, V, own, gw), f32),
        pltpu.VMEM((V, own, rows), f32),
        pltpu.VMEM((groups, V, own, gheads * rows), f32),
        pltpu.VMEM((groups, own, gheads * rows), f32),
        pltpu.VMEM((groups, tokens, gheads * rows), bf16),
        pltpu.VMEM((groups, tokens, gheads * rows), bf16),
        pltpu.VMEM((pieces, CORES, Y, Z, V, R, HD), f32),
        pltpu.VMEM((pieces, Y, Z, V, R, HD), f32),
        pltpu.VMEM((pieces, Y, Z, V, R, HD), f32),
        pltpu.VMEM((pieces, Y - 1, Z, V, R, HD), f32),
        pltpu.VMEM((pieces, Z, V, R, HD), f32),
        pltpu.VMEM((pieces, Z - 1, V, R, HD), f32),
        pltpu.VMEM((pieces, V, R, HD), f32),
        pltpu.VMEM((pieces, V, R, HD), f32),
        pltpu.VMEM((groups, rows, gheads * HD), bf16),
        pltpu.VMEM((groups, rows, gheads * HD), bf16),
        dma((2 + 2 * groups,)),
        dma((groups, 2)),
        dma((2, V - 1)), dma((2, V - 1)), dma((2, V - 1)), dma((2, V - 1)),
        dma((pieces,)), dma((pieces,)),
        dma((pieces, Y - 1)), dma((pieces, Y - 1)),
        dma((pieces, Z - 1)), dma((pieces, Z - 1)),
        dma((pieces, V - 1)), dma((pieces, V - 1)),
    ]
    shapes = (
        jax.ShapeDtypeStruct((rows, heads * HD), bf16),
        jax.ShapeDtypeStruct((rows, heads * HD), bf16),
        jax.ShapeDtypeStruct((R, G * HD), bf16),
        jax.ShapeDtypeStruct((R, G * HD), bf16),
    )
    results = pl.pallas_call(
        functools.partial(kernel, T, V),
        out_shape=shapes,
        in_specs=[hbm, hbm, hbm, hbm, vmem, smem],
        out_specs=(hbm, hbm, vmem, vmem),
        scratch_shapes=scratch,
        compiler_params=pltpu.CompilerParams(
            collective_id=0, has_side_effects=True, vmem_limit_bytes=56 * 1024 * 1024
        ),
        cost_estimate=pl.CostEstimate(
            flops=12 * rows * heads * tokens * HD,
            bytes_accessed=8 * rows * heads * HD + 4 * own * G * HD,
            transcendentals=rows * heads * tokens,
        ),
        name="attention",
    )(queries, grad_out, video_keys, video_values, positions.reshape(1, rows), span_bounds)
    return pl.pallas_call(
        hand_on,
        out_shape=shapes,
        in_specs=[hbm] * 4,
        out_specs=(hbm,) * 4,
        scratch_shapes=[dma((4,))],
        name="hand_on",
    )(*results)


def solution(mesh):
    placed = (
        P("text", None),
        P("video", None),
        P("video", None),
        P("text", None),
        P("text"),
        P("text", None),
    )
    return jax.shard_map(
        functools.partial(local, mesh.shape["text"], mesh.shape["video"]),
        mesh=mesh,
        in_specs=placed,
        out_specs=(
            P("text", "video"),
            P("text", "video"),
            P(("video", "text"), None),
            P(("video", "text"), None),
        ),
        check_vma=False,
    )
```

time: 41.6 us -> 68.6 us (1.65)
  Pallas kernels: 36.6 us -> 67.8 us
  local copies, waits for them, and re-layouts: 4.07 us -> 0 us
    pallas_call x1 -> x2, Pallas kernels: 36.6 us -> 67.8 us  [the longest x1 33.9 us: local(): pl.pallas_call(functools.partial(kernel, T, V), out_shape=shapes, in_spec...]
    unnamed x10 -> x0, local copies, waits for them, and re-layouts: 4.07 us -> none
where the time goes in v2:
time: 68.6 us; the launch traced here: 68.5 us
  Pallas kernels  67.8 us (99%)
    pallas_call x1, Pallas kernels, local(): pl.pallas_call(functools.partial(kernel, T, V), out_shape=shapes, in_spec...  33.9 us
    pallas_call x1, Pallas kernels, local(): pl.pallas_call(hand_on, out_shape=shapes, in_specs=[hbm] * 4, out_specs=(...  33.9 us

profile of v2, /device:TPU:0, one launch (start us, length us, event | category | flops | bytes accessed | tf_op | source)
XLA Modules:
  0.0 68.5 jit_solution(16496774797358263739)
XLA Ops:
  0.6 33.9 %attention.1 = (bf16[128,2048]{1,0:T(8,128)(2,1)}, bf16[128,2048]{1,0:T(8,128)(2,1)}, bf16[16,512]{1,0:T(8,128)(2,1)}, bf16[16,512]{1,0:T(8,128)(2,1)}) custom-call(bf16[128,4096]{1,0:T(8,128)(2,1)} %q_ref.1, bf16[128,4096]{1,0:T(8,128)(2,1)} %go_ref.1, bf16[256,512]{1,0:T(8,128)(2,1)} %k_ref.1, bf16[256,512]{1,0:T(8,128)(2,1)} %v_ref.1, s32[1,128]{1,0:T(1,128)} %bitcast.1, ...), custom_call_target="tpu_custom_call" | custom-call | flops 1610612736 | bytes 2621440 | tf_op jit(solution)/shard_map/attention/pallas_call | solution.py:361
  34.6 33.9 %hand_on.1 = (bf16[128,2048]{1,0:T(8,128)(2,1)}, bf16[128,2048]{1,0:T(8,128)(2,1)}, bf16[16,512]{1,0:T(8,128)(2,1)}, bf16[16,512]{1,0:T(8,128)(2,1)}) custom-call(bf16[128,2048]{1,0:T(8,128)(2,1)} %get-tuple-element.8.refs_0_, bf16[128,2048]{1,0:T(8,128)(2,1)} %get-tuple-element.9.refs_1_, bf16[16,512]{1,0:T(8,128)(2,1)} %get-tuple-element.10.refs_2_, ...), custom_call_target="tpu_custom_call" | custom-call | tf_op jit(solution)/shard_map/hand_on/pallas_call | solution.py:377

commit v3 on v2

--- a/solution.py
+++ b/solution.py
@@ -203,6 +203,13 @@
     def head_rows(ref, gi, first, count):
         return jnp.concatenate([ref[gi, :, h * HD : (h + 1) * HD] for h in range(first, first + count)], axis=0)
 
+    def pair_columns(pair):
+        return pl.ds(pl.multiple_of(pair * 2 * HD, 2 * HD), 2 * HD)
+
+    def head_pair(ref, gi, there):
+        both = ref[gi, :, there]
+        return jnp.concatenate([both[:, :HD], both[:, HD:]], axis=0)
+
     def key_rows(i, gi, j):
         return kv_all[i, j, :, gi * HD : (gi + 1) * HD].astype(bf16)
 
@@ -213,20 +220,24 @@
     for gi in range(groups):
         keys = key_rows(0, gi, 0)
         values = key_rows(1, gi, 0)
-        for pair in range(pairs):
-            there = slice(pair * 2 * HD, (pair + 1) * 2 * HD)
-            s_all[gi, 0, :, there] = scores(keys, head_rows(q_s, gi, 2 * pair, 2), 0)
+
+        @pl.loop(0, pairs)
+        def _(pair):
+            there = pair_columns(pair)
+            s_all[gi, 0, :, there] = scores(keys, head_pair(q_s, gi, there), 0)
             dp_own[gi, :, there] = lax.dot_general(
-                values, head_rows(go_s, gi, 2 * pair, 2), NT, preferred_element_type=f32
+                values, head_pair(go_s, gi, there), NT, preferred_element_type=f32
             )
 
     forward(0)
     collect(0)
     for gi in range(groups):
         keys = [key_rows(0, gi, j) for j in range(V)]
-        for pair in range(pairs):
-            there = slice(pair * 2 * HD, (pair + 1) * 2 * HD)
-            queries = head_rows(q_s, gi, 2 * pair, 2)
+
+        @pl.loop(0, pairs)
+        def _(pair):
+            there = pair_columns(pair)
+            queries = head_pair(q_s, gi, there)
             s = [s_all[gi, 0, :, there]] + [scores(keys[j], queries, j) for j in range(1, V)]
             peak = functools.reduce(jnp.maximum, [jnp.max(x, axis=0, keepdims=True) for x in s])
             e = [jnp.exp2(x - peak) for x in s]
@@ -235,8 +246,8 @@
                 prob = e[j] * inverse
                 s_all[gi, j, :, there] = prob
                 p_all[gi, j * own : (j + 1) * own, there] = prob.astype(bf16)
-            if gi > 0 and pair == pairs // 2 - 1:
-                tick()
+
+        tick()
         grad = jnp.dot(p_all[gi], head_rows(go_s, gi, 0, gheads), preferred_element_type=f32)
         launch(gi, grad)
         if gi == 0:
@@ -248,9 +259,11 @@
         kt = jnp.concatenate([kv_all[0, j, :, gi * HD : (gi + 1) * HD].T for j in range(V)], axis=1).astype(bf16)
         vt = jnp.concatenate([kv_all[1, j, :, gi * HD : (gi + 1) * HD].T for j in range(V)], axis=1).astype(bf16)
         values = [key_rows(1, gi, j) for j in range(V)]
-        for pair in range(pairs):
-            there = slice(pair * 2 * HD, (pair + 1) * 2 * HD)
-            gp = head_rows(go_s, gi, 2 * pair, 2)
+
+        @pl.loop(0, pairs)
+        def _(pair):
+            there = pair_columns(pair)
+            gp = head_pair(go_s, gi, there)
             dprob = [dp_own[gi, :, there]] + [
                 lax.dot_general(values[j], gp, NT, preferred_element_type=f32) for j in range(1, V)
             ]
@@ -260,12 +273,10 @@
                 ds_all[gi, j * own : (j + 1) * own, there] = (prob[j] * (dprob[j] - delta)).astype(bf16)
             out = jnp.dot(vt, p_all[gi, :, there], preferred_element_type=f32).T.astype(bf16)
             dq = (jnp.dot(kt, ds_all[gi, :, there], preferred_element_type=f32) * scale).T.astype(bf16)
-            for i in range(2):
-                h = 2 * pair + i
-                att_s[gi, :, h * HD : (h + 1) * HD] = out[i * HD : (i + 1) * HD]
-                dq_s[gi, :, h * HD : (h + 1) * HD] = dq[i * HD : (i + 1) * HD]
-            if pair == pairs // 2 - 1:
-                tick()
+            att_s[gi, :, there] = jnp.concatenate([out[:HD], out[HD:]], axis=1)
+            dq_s[gi, :, there] = jnp.concatenate([dq[:HD], dq[HD:]], axis=1)
+
+        tick()
         grad = jnp.dot(ds_all[gi], head_rows(q_s, gi, 0, gheads), preferred_element_type=f32) * scale
         launch(groups + gi, grad)
         cols = slice(gi * gheads * HD, (gi + 1) * gheads * HD)
@@ -296,12 +307,15 @@
 
 
 def hand_on(*refs):
-    count = (len(refs) - 1) // 2
-    sems = refs[-1]
-    copies = [pltpu.make_async_copy(refs[i], refs[count + i], sems.at[i]) for i in range(count)]
-    for copy in copies:
+    sources, results, held, sems = refs[:4], refs[4:8], refs[8:12], refs[12]
+    arrivals = [pltpu.make_async_copy(sources[i], held[i], sems.at[0, i]) for i in range(4)]
+    departures = [pltpu.make_async_copy(held[i], results[i], sems.at[1, i]) for i in range(4)]
+    for copy in arrivals:
         copy.start()
-    for copy in copies:
+    for arrival, departure in zip(arrivals, departures):
+        arrival.wait()
+        departure.start()
+    for copy in departures:
         copy.wait()
 
 
@@ -379,7 +393,7 @@
         out_shape=shapes,
         in_specs=[hbm] * 4,
         out_specs=(hbm,) * 4,
-        scratch_shapes=[dma((4,))],
+        scratch_shapes=[pltpu.VMEM(shape.shape, bf16) for shape in shapes] + [dma((2, 4))],
         name="hand_on",
     )(*results)
 

time: 68.6 us -> 39.4 us (0.57)
  Pallas kernels: 67.8 us -> 38.6 us
    pallas_call x1, Pallas kernels: 33.9 us -> 2.08 us  [local(): pl.pallas_call(hand_on, out_shape=shapes, in_specs=[hbm] * 4, out_specs=(...]
    pallas_call x1, Pallas kernels: 33.9 us -> 36.5 us  [local(): pl.pallas_call(functools.partial(kernel, T, V), out_shape=shapes, in_spec...]
where the time goes in v3:
time: 39.4 us; the launch traced here: 39.2 us
  Pallas kernels  38.6 us (98%)
  between operations  0.64 us (2%)
    pallas_call x1, Pallas kernels, local(): pl.pallas_call(functools.partial(kernel, T, V), out_shape=shapes, in_spec...  36.5 us
    pallas_call x1, Pallas kernels, local(): pl.pallas_call(hand_on, out_shape=shapes, in_specs=[hbm] * 4, out_specs=(...  2.08 us

profile of v3, /device:TPU:0, one launch (start us, length us, event | category | flops | bytes accessed | tf_op | source)
XLA Modules:
  0.0 39.2 jit_solution(5424944933462010449)
XLA Ops:
  0.6 36.5 %attention.1 = (bf16[128,2048]{1,0:T(8,128)(2,1)}, bf16[128,2048]{1,0:T(8,128)(2,1)}, bf16[16,512]{1,0:T(8,128)(2,1)}, bf16[16,512]{1,0:T(8,128)(2,1)}) custom-call(bf16[128,4096]{1,0:T(8,128)(2,1)} %q_ref.1, bf16[128,4096]{1,0:T(8,128)(2,1)} %go_ref.1, bf16[256,512]{1,0:T(8,128)(2,1)} %k_ref.1, bf16[256,512]{1,0:T(8,128)(2,1)} %v_ref.1, s32[1,128]{1,0:T(1,128)} %bitcast.1, ...), custom_call_target="tpu_custom_call" | custom-call | flops 1610612736 | bytes 2621440 | tf_op jit(solution)/shard_map/attention/pallas_call | solution.py:375
  37.1 2.1 %hand_on.1 = (bf16[128,2048]{1,0:T(8,128)(2,1)}, bf16[128,2048]{1,0:T(8,128)(2,1)}, bf16[16,512]{1,0:T(8,128)(2,1)}, bf16[16,512]{1,0:T(8,128)(2,1)}) custom-call(bf16[128,2048]{1,0:T(8,128)(2,1)} %get-tuple-element.8.refs_0_, bf16[128,2048]{1,0:T(8,128)(2,1)} %get-tuple-element.9.refs_1_, bf16[16,512]{1,0:T(8,128)(2,1)} %get-tuple-element.10.refs_2_, ...), custom_call_target="tpu_custom_call" | custom-call | tf_op jit(solution)/shard_map/hand_on/pallas_call | solution.py:391

commit v4 on v3

--- a/solution.py
+++ b/solution.py
@@ -34,9 +34,9 @@
     T, V, q_ref, go_ref, k_ref, v_ref, pos_ref, span_ref,
     att_ref, dq_ref, dk_ref, dv_ref,
     q_s, go_s, kv_s, kv_out, kv_in, kv_all, bias, s_all, dp_own, p_all, ds_all,
-    part, r_core, s_y, r_y, s_z, r_z, s_x, r_x, att_s, dq_s,
+    part, r_core, s_y, r_y, s_z, r_z, att_s, dq_s,
     load_sem, out_sem, kv_send, kv_recv, fw_send, fw_recv,
-    c_send, c_recv, y_send, y_recv, z_send, z_recv, x_send, x_recv,
+    c_send, c_recv, y_send, y_recv, z_send, z_recv,
 ):
     Z = DEPTH
     Y = T // (CORES * Z)
@@ -79,9 +79,10 @@
 
     barrier = pltpu.get_barrier_semaphore()
     partners = [(sib, v)]
-    partners += [(t, lax.rem(v + k, V)) for k in range(1, V)]
     partners += [(text_at(z, lax.rem(y + k, Y)), v) for k in range(1, Y)]
-    partners += [(text_at(lax.rem(z + k, Z), y), v) for k in range(1, Z)]
+    partners += [
+        (text_at(lax.rem(z + k, Z), y), lax.rem(v + m, V)) for k in range(Z) for m in range(V) if k + m > 0
+    ]
     for partner in partners:
         pl.semaphore_signal(barrier, inc=1, device_id=partner, device_id_type=MESH)
 
@@ -138,36 +139,26 @@
             copies.append(copy)
         return copies
 
-    def start_z(p, before):
+    def start_zx(p, before):
         total = s_y[p, y]
         for k in range(1, Y):
             before[k - 1].wait_recv()
             total += r_y[p, k - 1]
         s_z[p] = total
         copies = []
-        for k in range(1, Z):
-            zz = lax.rem(z + k, Z)
-            copy = remote(s_z.at[p, zz], r_z.at[p, k - 1], z_send.at[p, k - 1], z_recv.at[p, k - 1], text_at(zz, y), v)
-            copy.start()
-            copies.append(copy)
+        for k in range(Z):
+            for m in range(V):
+                if k + m > 0:
+                    zz, vv, at = lax.rem(z + k, Z), lax.rem(v + m, V), k * V + m - 1
+                    copy = remote(
+                        s_z.at[p, zz, vv], r_z.at[p, k, v], z_send.at[p, at], z_recv.at[p, at], text_at(zz, y), vv
+                    )
+                    copy.start()
+                    copies.append(copy)
+        r_z[p, 0, v] = s_z[p, z, v]
         return copies
 
-    def start_x(p, before):
-        total = s_z[p, z]
-        for k in range(1, Z):
-            before[k - 1].wait_recv()
-            total += r_z[p, k - 1]
-        s_x[p] = total
-        copies = []
-        for k in range(1, V):
-            vv = lax.rem(v + k, V)
-            copy = remote(s_x.at[p, vv], r_x.at[p, v], x_send.at[p, k - 1], x_recv.at[p, k - 1], t, vv)
-            copy.start()
-            copies.append(copy)
-        r_x[p, v] = s_x[p, v]
-        return copies
-
-    stages = (start_y, start_z, start_x)
+    stages = (start_y, start_zx)
 
     def launch(p, grad):
         for j in range(V):
@@ -198,46 +189,39 @@
     for load in loads[2:]:
         load.wait()
 
-    pairs = gheads // 2
+    unit = min(4, gheads)
+    units = gheads // unit
+
+    def unit_columns(n):
+        return slice(n * unit * HD, (n + 1) * unit * HD)
 
     def head_rows(ref, gi, first, count):
         return jnp.concatenate([ref[gi, :, h * HD : (h + 1) * HD] for h in range(first, first + count)], axis=0)
 
-    def pair_columns(pair):
-        return pl.ds(pl.multiple_of(pair * 2 * HD, 2 * HD), 2 * HD)
-
-    def head_pair(ref, gi, there):
-        both = ref[gi, :, there]
-        return jnp.concatenate([both[:, :HD], both[:, HD:]], axis=0)
-
     def key_rows(i, gi, j):
         return kv_all[i, j, :, gi * HD : (gi + 1) * HD].astype(bf16)
 
     def scores(keys, queries, j):
         raw = lax.dot_general(keys, queries, NT, preferred_element_type=f32)
-        return raw * (scale * math.log2(math.e)) + jnp.concatenate([bias[j]] * 2, axis=1)
+        return raw * (scale * math.log2(math.e)) + jnp.concatenate([bias[j]] * unit, axis=1)
 
     for gi in range(groups):
         keys = key_rows(0, gi, 0)
         values = key_rows(1, gi, 0)
-
-        @pl.loop(0, pairs)
-        def _(pair):
-            there = pair_columns(pair)
-            s_all[gi, 0, :, there] = scores(keys, head_pair(q_s, gi, there), 0)
+        for n in range(units):
+            there = unit_columns(n)
+            s_all[gi, 0, :, there] = scores(keys, head_rows(q_s, gi, n * unit, unit), 0)
             dp_own[gi, :, there] = lax.dot_general(
-                values, head_pair(go_s, gi, there), NT, preferred_element_type=f32
+                values, head_rows(go_s, gi, n * unit, unit), NT, preferred_element_type=f32
             )
 
     forward(0)
     collect(0)
     for gi in range(groups):
         keys = [key_rows(0, gi, j) for j in range(V)]
-
-        @pl.loop(0, pairs)
-        def _(pair):
-            there = pair_columns(pair)
-            queries = head_pair(q_s, gi, there)
+        for n in range(units):
+            there = unit_columns(n)
+            queries = head_rows(q_s, gi, n * unit, unit)
             s = [s_all[gi, 0, :, there]] + [scores(keys[j], queries, j) for j in range(1, V)]
             peak = functools.reduce(jnp.maximum, [jnp.max(x, axis=0, keepdims=True) for x in s])
             e = [jnp.exp2(x - peak) for x in s]
@@ -246,24 +230,19 @@
                 prob = e[j] * inverse
                 s_all[gi, j, :, there] = prob
                 p_all[gi, j * own : (j + 1) * own, there] = prob.astype(bf16)
-
-        tick()
+            if n == 0:
+                tick()
         grad = jnp.dot(p_all[gi], head_rows(go_s, gi, 0, gheads), preferred_element_type=f32)
         launch(gi, grad)
         if gi == 0:
             forward(1)
 
     collect(1)
-    outs = []
     for gi in range(groups):
-        kt = jnp.concatenate([kv_all[0, j, :, gi * HD : (gi + 1) * HD].T for j in range(V)], axis=1).astype(bf16)
-        vt = jnp.concatenate([kv_all[1, j, :, gi * HD : (gi + 1) * HD].T for j in range(V)], axis=1).astype(bf16)
         values = [key_rows(1, gi, j) for j in range(V)]
-
-        @pl.loop(0, pairs)
-        def _(pair):
-            there = pair_columns(pair)
-            gp = head_pair(go_s, gi, there)
+        for n in range(units):
+            there = unit_columns(n)
+            gp = head_rows(go_s, gi, n * unit, unit)
             dprob = [dp_own[gi, :, there]] + [
                 lax.dot_general(values[j], gp, NT, preferred_element_type=f32) for j in range(1, V)
             ]
@@ -271,14 +250,26 @@
             delta = sum(jnp.sum(prob[j] * dprob[j], axis=0, keepdims=True) for j in range(V))
             for j in range(V):
                 ds_all[gi, j * own : (j + 1) * own, there] = (prob[j] * (dprob[j] - delta)).astype(bf16)
-            out = jnp.dot(vt, p_all[gi, :, there], preferred_element_type=f32).T.astype(bf16)
-            dq = (jnp.dot(kt, ds_all[gi, :, there], preferred_element_type=f32) * scale).T.astype(bf16)
-            att_s[gi, :, there] = jnp.concatenate([out[:HD], out[HD:]], axis=1)
-            dq_s[gi, :, there] = jnp.concatenate([dq[:HD], dq[HD:]], axis=1)
-
-        tick()
+            if n == 0:
+                tick()
         grad = jnp.dot(ds_all[gi], head_rows(q_s, gi, 0, gheads), preferred_element_type=f32) * scale
         launch(groups + gi, grad)
+
+    outs = []
+    for gi in range(groups):
+        kt = jnp.concatenate([kv_all[0, j, :, gi * HD : (gi + 1) * HD].T for j in range(V)], axis=1).astype(bf16)
+        vt = jnp.concatenate([kv_all[1, j, :, gi * HD : (gi + 1) * HD].T for j in range(V)], axis=1).astype(bf16)
+        for n in range(units):
+            there = unit_columns(n)
+            out = jnp.dot(vt, p_all[gi, :, there], preferred_element_type=f32)
+            dq = jnp.dot(kt, ds_all[gi, :, there], preferred_element_type=f32) * scale
+            for i in range(unit):
+                here = slice(i * HD, (i + 1) * HD)
+                h = n * unit + i
+                att_s[gi, :, h * HD : (h + 1) * HD] = out[:, here].T.astype(bf16)
+                dq_s[gi, :, h * HD : (h + 1) * HD] = dq[:, here].T.astype(bf16)
+            if n == 0:
+                tick()
         cols = slice(gi * gheads * HD, (gi + 1) * gheads * HD)
         for i, (src, dst) in enumerate(((att_s, att_ref), (dq_s, dq_ref))):
             copy = pltpu.make_async_copy(src.at[gi], dst.at[:, cols], out_sem.at[gi, i])
@@ -298,8 +289,8 @@
             share = V // G
             found = [(0, g * share + i) for i in range(share)]
         there = slice(g * HD, (g + 1) * HD)
-        dv_ref[:, there] = sum(r_x[gi, rank] for gi, rank in found).astype(bf16)
-        dk_ref[:, there] = sum(r_x[groups + gi, rank] for gi, rank in found).astype(bf16)
+        dv_ref[:, there] = sum(r_z[gi, k, rank] for gi, rank in found for k in range(Z)).astype(bf16)
+        dk_ref[:, there] = sum(r_z[groups + gi, k, rank] for gi, rank in found for k in range(Z)).astype(bf16)
     for copy in pending + sends[0] + sends[1] + forwards[0] + forwards[1]:
         copy.wait_send()
     for copy in outs:
@@ -308,8 +299,13 @@
 
 def hand_on(*refs):
     sources, results, held, sems = refs[:4], refs[4:8], refs[8:12], refs[12]
-    arrivals = [pltpu.make_async_copy(sources[i], held[i], sems.at[0, i]) for i in range(4)]
-    departures = [pltpu.make_async_copy(held[i], results[i], sems.at[1, i]) for i in range(4)]
+    arrivals, departures = [], []
+    for i in range(4):
+        chunk = max(32, sources[i].shape[0] // 4) if i < 2 else sources[i].shape[0]
+        for n in range(sources[i].shape[0] // chunk):
+            rows = pl.ds(n * chunk, chunk)
+            arrivals.append(pltpu.make_async_copy(sources[i].at[rows], held[i].at[rows], sems.at[0, i, n]))
+            departures.append(pltpu.make_async_copy(held[i].at[rows], results[i].at[rows], sems.at[1, i, n]))
     for copy in arrivals:
         copy.start()
     for arrival, departure in zip(arrivals, departures):
@@ -353,9 +349,7 @@
         pltpu.VMEM((pieces, Y, Z, V, R, HD), f32),
         pltpu.VMEM((pieces, Y - 1, Z, V, R, HD), f32),
         pltpu.VMEM((pieces, Z, V, R, HD), f32),
-        pltpu.VMEM((pieces, Z - 1, V, R, HD), f32),
-        pltpu.VMEM((pieces, V, R, HD), f32),
-        pltpu.VMEM((pieces, V, R, HD), f32),
+        pltpu.VMEM((pieces, Z, V, R, HD), f32),
         pltpu.VMEM((groups, rows, gheads * HD), bf16),
         pltpu.VMEM((groups, rows, gheads * HD), bf16),
         dma((2 + 2 * groups,)),
@@ -363,8 +357,7 @@
         dma((2, V - 1)), dma((2, V - 1)), dma((2, V - 1)), dma((2, V - 1)),
         dma((pieces,)), dma((pieces,)),
         dma((pieces, Y - 1)), dma((pieces, Y - 1)),
-        dma((pieces, Z - 1)), dma((pieces, Z - 1)),
-        dma((pieces, V - 1)), dma((pieces, V - 1)),
+        dma((pieces, Z * V - 1)), dma((pieces, Z * V - 1)),
     ]
     shapes = (
         jax.ShapeDtypeStruct((rows, heads * HD), bf16),
@@ -393,7 +386,7 @@
         out_shape=shapes,
         in_specs=[hbm] * 4,
         out_specs=(hbm,) * 4,
-        scratch_shapes=[pltpu.VMEM(shape.shape, bf16) for shape in shapes] + [dma((2, 4))],
+        scratch_shapes=[pltpu.VMEM(shape.shape, bf16) for shape in shapes] + [dma((2, 4, 4))],
         name="hand_on",
     )(*results)
 

time: 39.4 us -> 34.2 us (0.87)
  Pallas kernels: 38.6 us -> 33.4 us
    pallas_call x1, Pallas kernels: 36.5 us -> 31.1 us  [local(): pl.pallas_call(functools.partial(kernel, T, V), out_shape=shapes, in_spec...]
where the time goes in v4:
time: 34.2 us; the launch traced here: 34 us
  Pallas kernels  33.4 us (98%)
  between operations  0.64 us (2%)
    pallas_call x1, Pallas kernels, local(): pl.pallas_call(functools.partial(kernel, T, V), out_shape=shapes, in_spec...  31.1 us
    pallas_call x1, Pallas kernels, local(): pl.pallas_call(hand_on, out_shape=shapes, in_specs=[hbm] * 4, out_specs=(...  2.23 us

profile of v4, /device:TPU:0, one launch (start us, length us, event | category | flops | bytes accessed | tf_op | source)
XLA Modules:
  0.0 34.0 jit_solution(17764158643494484390)
XLA Ops:
  0.6 31.1 %attention.1 = (bf16[128,2048]{1,0:T(8,128)(2,1)}, bf16[128,2048]{1,0:T(8,128)(2,1)}, bf16[16,512]{1,0:T(8,128)(2,1)}, bf16[16,512]{1,0:T(8,128)(2,1)}) custom-call(bf16[128,4096]{1,0:T(8,128)(2,1)} %q_ref.1, bf16[128,4096]{1,0:T(8,128)(2,1)} %go_ref.1, bf16[256,512]{1,0:T(8,128)(2,1)} %k_ref.1, bf16[256,512]{1,0:T(8,128)(2,1)} %v_ref.1, s32[1,128]{1,0:T(1,128)} %bitcast.1, ...), custom_call_target="tpu_custom_call" | custom-call | flops 1610612736 | bytes 2621440 | tf_op jit(solution)/shard_map/attention/pallas_call | solution.py:368
  31.8 2.2 %hand_on.1 = (bf16[128,2048]{1,0:T(8,128)(2,1)}, bf16[128,2048]{1,0:T(8,128)(2,1)}, bf16[16,512]{1,0:T(8,128)(2,1)}, bf16[16,512]{1,0:T(8,128)(2,1)}) custom-call(bf16[128,2048]{1,0:T(8,128)(2,1)} %get-tuple-element.8.refs_0_, bf16[128,2048]{1,0:T(8,128)(2,1)} %get-tuple-element.9.refs_1_, bf16[16,512]{1,0:T(8,128)(2,1)} %get-tuple-element.10.refs_2_, ...), custom_call_target="tpu_custom_call" | custom-call | tf_op jit(solution)/shard_map/hand_on/pallas_call | solution.py:384

commit v5 on v4

--- a/solution.py
+++ b/solution.py
@@ -33,7 +33,7 @@
 def kernel(
     T, V, q_ref, go_ref, k_ref, v_ref, pos_ref, span_ref,
     att_ref, dq_ref, dk_ref, dv_ref,
-    q_s, go_s, kv_s, kv_out, kv_in, kv_all, bias, s_all, dp_own, p_all, ds_all,
+    q_s, go_s, kv_s, kv_out, kv_in, kv_all, bias, s_all, dp_own, own_peak, own_total, weights, p_all, ds_all,
     part, r_core, s_y, r_y, s_z, r_z, att_s, dq_s,
     load_sem, out_sem, kv_send, kv_recv, fw_send, fw_recv,
     c_send, c_recv, y_send, y_recv, z_send, z_recv,
@@ -205,12 +205,19 @@
         raw = lax.dot_general(keys, queries, NT, preferred_element_type=f32)
         return raw * (scale * math.log2(math.e)) + jnp.concatenate([bias[j]] * unit, axis=1)
 
+    def exponentials(s):
+        peak = jnp.max(s, axis=0, keepdims=True)
+        e = jnp.exp2(s - peak)
+        return e, peak, jnp.sum(e, axis=0, keepdims=True)
+
     for gi in range(groups):
         keys = key_rows(0, gi, 0)
         values = key_rows(1, gi, 0)
         for n in range(units):
             there = unit_columns(n)
-            s_all[gi, 0, :, there] = scores(keys, head_rows(q_s, gi, n * unit, unit), 0)
+            s_all[gi, 0, :, there], own_peak[gi, :, there], own_total[gi, :, there] = exponentials(
+                scores(keys, head_rows(q_s, gi, n * unit, unit), 0)
+            )
             dp_own[gi, :, there] = lax.dot_general(
                 values, head_rows(go_s, gi, n * unit, unit), NT, preferred_element_type=f32
             )
@@ -222,14 +229,21 @@
         for n in range(units):
             there = unit_columns(n)
             queries = head_rows(q_s, gi, n * unit, unit)
-            s = [s_all[gi, 0, :, there]] + [scores(keys[j], queries, j) for j in range(1, V)]
-            peak = functools.reduce(jnp.maximum, [jnp.max(x, axis=0, keepdims=True) for x in s])
-            e = [jnp.exp2(x - peak) for x in s]
-            inverse = 1.0 / sum(jnp.sum(x, axis=0, keepdims=True) for x in e)
+            e, peaks, totals = [None], [own_peak[gi, :, there]], [own_total[gi, :, there]]
+            for j in range(1, V):
+                block, peak, total = exponentials(scores(keys[j], queries, j))
+                s_all[gi, j, :, there] = block
+                e.append(block)
+                peaks.append(peak)
+                totals.append(total)
+            e[0] = s_all[gi, 0, :, there]
+            top = functools.reduce(jnp.maximum, peaks)
+            shrink = [jnp.exp2(peak - top) for peak in peaks]
+            inverse = 1.0 / sum(total * factor for total, factor in zip(totals, shrink))
             for j in range(V):
-                prob = e[j] * inverse
-                s_all[gi, j, :, there] = prob
-                p_all[gi, j * own : (j + 1) * own, there] = prob.astype(bf16)
+                weight = shrink[j] * inverse
+                weights[gi, j, :, there] = weight
+                p_all[gi, j * own : (j + 1) * own, there] = (e[j] * weight).astype(bf16)
             if n == 0:
                 tick()
         grad = jnp.dot(p_all[gi], head_rows(go_s, gi, 0, gheads), preferred_element_type=f32)
@@ -246,10 +260,14 @@
             dprob = [dp_own[gi, :, there]] + [
                 lax.dot_general(values[j], gp, NT, preferred_element_type=f32) for j in range(1, V)
             ]
-            prob = [s_all[gi, j, :, there] for j in range(V)]
-            delta = sum(jnp.sum(prob[j] * dprob[j], axis=0, keepdims=True) for j in range(V))
+            weight = [weights[gi, j, :, there] for j in range(V)]
+            delta = sum(
+                jnp.sum(s_all[gi, j, :, there] * dprob[j], axis=0, keepdims=True) * weight[j] for j in range(V)
+            )
             for j in range(V):
-                ds_all[gi, j * own : (j + 1) * own, there] = (prob[j] * (dprob[j] - delta)).astype(bf16)
+                ds_all[gi, j * own : (j + 1) * own, there] = (
+                    s_all[gi, j, :, there] * ((dprob[j] - delta) * weight[j])
+                ).astype(bf16)
             if n == 0:
                 tick()
         grad = jnp.dot(ds_all[gi], head_rows(q_s, gi, 0, gheads), preferred_element_type=f32) * scale
@@ -298,20 +316,10 @@
 
 
 def hand_on(*refs):
-    sources, results, held, sems = refs[:4], refs[4:8], refs[8:12], refs[12]
-    arrivals, departures = [], []
-    for i in range(4):
-        chunk = max(32, sources[i].shape[0] // 4) if i < 2 else sources[i].shape[0]
-        for n in range(sources[i].shape[0] // chunk):
-            rows = pl.ds(n * chunk, chunk)
-            arrivals.append(pltpu.make_async_copy(sources[i].at[rows], held[i].at[rows], sems.at[0, i, n]))
-            departures.append(pltpu.make_async_copy(held[i].at[rows], results[i].at[rows], sems.at[1, i, n]))
-    for copy in arrivals:
+    copies = [pltpu.make_async_copy(refs[i], refs[4 + i], refs[8].at[i]) for i in range(4)]
+    for copy in copies:
         copy.start()
-    for arrival, departure in zip(arrivals, departures):
-        arrival.wait()
-        departure.start()
-    for copy in departures:
+    for copy in copies:
         copy.wait()
 
 
@@ -342,6 +350,9 @@
         pltpu.VMEM((V, own, rows), f32),
         pltpu.VMEM((groups, V, own, gheads * rows), f32),
         pltpu.VMEM((groups, own, gheads * rows), f32),
+        pltpu.VMEM((groups, 1, gheads * rows), f32),
+        pltpu.VMEM((groups, 1, gheads * rows), f32),
+        pltpu.VMEM((groups, V, 1, gheads * rows), f32),
         pltpu.VMEM((groups, tokens, gheads * rows), bf16),
         pltpu.VMEM((groups, tokens, gheads * rows), bf16),
         pltpu.VMEM((pieces, CORES, Y, Z, V, R, HD), f32),
@@ -367,7 +378,7 @@
     )
     results = pl.pallas_call(
         functools.partial(kernel, T, V),
-        out_shape=shapes,
+        out_shape=tuple(pltpu.VMEM(shape.shape, bf16) for shape in shapes),
         in_specs=[hbm, hbm, hbm, hbm, vmem, smem],
         out_specs=(hbm, hbm, vmem, vmem),
         scratch_shapes=scratch,
@@ -386,7 +397,7 @@
         out_shape=shapes,
         in_specs=[hbm] * 4,
         out_specs=(hbm,) * 4,
-        scratch_shapes=[pltpu.VMEM(shape.shape, bf16) for shape in shapes] + [dma((2, 4, 4))],
+        scratch_shapes=[dma((4,))],
         name="hand_on",
     )(*results)
 

time: 34.2 us -> 67.8 us (1.98)
  Pallas kernels: 33.4 us -> 64.2 us
  local copies, waits for them, and re-layouts: 0 us -> 2.78 us
    pallas_call x1, Pallas kernels: 2.23 us -> 33.9 us  [local(): pl.pallas_call(hand_on, out_shape=shapes, in_specs=[hbm] * 4, out_specs=(...]
    unnamed x0 -> x8, local copies, waits for them, and re-layouts: none -> 2.78 us
    pallas_call x1, Pallas kernels: 31.1 us -> 30.3 us  [local(): pl.pallas_call(functools.partial(kernel, T, V), out_shape=tuple((pltpu.VM...]
where the time goes in v5:
time: 67.8 us; the launch traced here: 67.7 us
  Pallas kernels  64.2 us (95%)
  local copies, waits for them, and re-layouts  2.78 us (4%)
    pallas_call x1, Pallas kernels, local(): pl.pallas_call(hand_on, out_shape=shapes, in_specs=[hbm] * 4, out_specs=(...  33.9 us
    pallas_call x1, Pallas kernels, local(): pl.pallas_call(functools.partial(kernel, T, V), out_shape=tuple((pltpu.VM...  30.3 us
    unnamed x8, local copies, waits for them, and re-layouts  2.78 us

profile of v5, /device:TPU:0, one launch (start us, length us, event | category | flops | bytes accessed | tf_op | source)
XLA Modules:
  0.0 67.7 jit_solution(11522035001313827585)
XLA Ops:
  0.6 30.3 %attention.1 = (bf16[128,2048]{1,0:T(8,128)(2,1)S(1)}, bf16[128,2048]{1,0:T(8,128)(2,1)S(1)}, bf16[16,512]{1,0:T(8,128)(2,1)S(1)}, bf16[16,512]{1,0:T(8,128)(2,1)S(1)}) custom-call(bf16[128,4096]{1,0:T(8,128)(2,1)} %q_ref.1, bf16[128,4096]{1,0:T(8,128)(2,1)} %go_ref.1, bf16[256,512]{1,0:T(8,128)(2,1)} %k_ref.1, bf16[256,512]{1,0:T(8,128)(2,1)} %v_ref.1, ...), custom_call_target="tpu_custom_call" | custom-call | flops 1610612736 | bytes 2621440 | tf_op jit(solution)/shard_map/attention/pallas_call | solution.py:379
  31.0 0.0 copy-start
  31.0 0.8 %copy-done = bf16[128,2048]{1,0:T(8,128)(2,1)} copy-done((bf16[128,2048]{1,0:T(8,128)(2,1)}, bf16[128,2048]{1,0:T(8,128)(2,1)S(1)}, u32[]{:S(2)}) %copy-start) | copy-done | bytes 524312
  31.8 0.0 copy-start.1
  31.8 0.8 %copy-done.1 = bf16[128,2048]{1,0:T(8,128)(2,1)} copy-done((bf16[128,2048]{1,0:T(8,128)(2,1)}, bf16[128,2048]{1,0:T(8,128)(2,1)S(1)}, u32[]{:S(2)}) %copy-start.1) | copy-done | bytes 524312
  32.6 0.0 copy-start.2
  32.6 0.6 copy-done.2
  33.2 0.0 copy-start.3
  33.2 0.6 copy-done.3
  33.8 33.9 %hand_on.1 = (bf16[128,2048]{1,0:T(8,128)(2,1)}, bf16[128,2048]{1,0:T(8,128)(2,1)}, bf16[16,512]{1,0:T(8,128)(2,1)}, bf16[16,512]{1,0:T(8,128)(2,1)}) custom-call(bf16[128,2048]{1,0:T(8,128)(2,1)} %copy-done, bf16[128,2048]{1,0:T(8,128)(2,1)} %copy-done.1, bf16[16,512]{1,0:T(8,128)(2,1)} %copy-done.2, bf16[16,512]{1,0:T(8,128)(2,1)} %copy-done.3), custom_call_target="tpu_custom_call" | custom-call | tf_op jit(solution)/shard_map/hand_on/pallas_call | solution.py:395
Async XLA Ops:
  31.0 0.8 %copy-start = (bf16[128,2048]{1,0:T(8,128)(2,1)}, bf16[128,2048]{1,0:T(8,128)(2,1)S(1)}, u32[]{:S(2)}) copy-start(bf16[128,2048]{1,0:T(8,128)(2,1)S(1)} %get-tuple-element.8.refs_0_) | copy-start | bytes 1572868
  31.8 0.8 %copy-start.1 = (bf16[128,2048]{1,0:T(8,128)(2,1)}, bf16[128,2048]{1,0:T(8,128)(2,1)S(1)}, u32[]{:S(2)}) copy-start(bf16[128,2048]{1,0:T(8,128)(2,1)S(1)} %get-tuple-element.9.refs_1_) | copy-start | bytes 1572868
  32.6 0.6 copy-start.2
  33.2 0.6 copy-start.3

commit v6 on v5

--- a/solution.py
+++ b/solution.py
@@ -45,7 +45,6 @@
     gheads = heads // groups
     own = kv_s.shape[1]
     half = own // CORES
-    gw = groups * HD
     R = own // T
     scale = HD ** -0.5
     f32, bf16 = jnp.float32, jnp.bfloat16
@@ -60,8 +59,8 @@
     def text_at(zz, yy):
         return (zz * Y + yy) * CORES + c
 
-    def key_column(rank):
-        return pl.multiple_of(((rank * heads) // PER_GROUP) * HD, HD)
+    def key_column(rank, gi):
+        return pl.multiple_of(((rank * heads) // PER_GROUP + gi) * HD, HD)
 
     def source(k):
         return lax.rem(v - k + V, V)
@@ -90,35 +89,33 @@
     loads[1].wait()
     rows = pl.ds(pl.multiple_of(c * half, half), half)
     rest = pl.ds(pl.multiple_of((1 - c) * half, half), half)
-    for k in range(1, V):
-        cols = pl.ds(key_column(lax.rem(v + k, V)), gw)
-        for i in range(2):
-            kv_out[i, k - 1] = kv_s[i, rows, cols].astype(f32)
+    for i in range(2):
+        for gi in range(groups):
+            for k in range(1, V):
+                kv_out[i, gi, k - 1] = kv_s[i, rows, pl.ds(key_column(lax.rem(v + k, V), gi), HD)].astype(f32)
     pl.semaphore_wait(barrier, len(partners))
-    sends = [[], []]
+    sends, forwards = {}, {}
     for i in range(2):
+        for gi in range(groups):
+            for k in range(1, V):
+                at = (i, gi, k - 1)
+                copy = remote(kv_out.at[at], kv_in.at[(*at, c)], kv_send.at[at], kv_recv.at[at], t, lax.rem(v + k, V))
+                copy.start()
+                sends[at] = copy
+
+    def forward(i, gi):
         for k in range(1, V):
-            copy = remote(
-                kv_out.at[i, k - 1], kv_in.at[i, k - 1, c], kv_send.at[i, k - 1], kv_recv.at[i, k - 1], t, lax.rem(v + k, V)
-            )
+            at = (i, gi, k - 1)
+            sends[at].wait_recv()
+            copy = remote(kv_in.at[(*at, c)], kv_in.at[(*at, c)], fw_send.at[at], fw_recv.at[at], sib, v)
             copy.start()
-            sends[i].append(copy)
-    forwards = [[], []]
-
-    def forward(i):
+            forwards[at] = copy
+            kv_all[i, gi, k, rows, :] = kv_in[i, gi, k - 1, c]
+
+    def collect(i, gi):
         for k in range(1, V):
-            sends[i][k - 1].wait_recv()
-            copy = remote(
-                kv_in.at[i, k - 1, c], kv_in.at[i, k - 1, c], fw_send.at[i, k - 1], fw_recv.at[i, k - 1], sib, v
-            )
-            copy.start()
-            forwards[i].append(copy)
-            kv_all[i, k, rows, :] = kv_in[i, k - 1, c]
-
-    def collect(i):
-        for k in range(1, V):
-            forwards[i][k - 1].wait_recv()
-            kv_all[i, k, rest, :] = kv_in[i, k - 1, 1 - c]
+            forwards[i, gi, k - 1].wait_recv()
+            kv_all[i, gi, k, rest, :] = kv_in[i, gi, k - 1, 1 - c]
 
     pending = []
     flying = []
@@ -183,9 +180,9 @@
     for j in range(V):
         token = source(j) * own + lax.broadcasted_iota(jnp.int32, (own, HD), 0)
         bias[j] = jnp.where((token >= low) & (token < high) & (token <= pos), 0.0, FLOOR)
-    cols = pl.ds(key_column(v), gw)
     for i in range(2):
-        kv_all[i, 0] = kv_s[i, :, cols].astype(f32)
+        for gi in range(groups):
+            kv_all[i, gi, 0] = kv_s[i, :, pl.ds(key_column(v, gi), HD)].astype(f32)
     for load in loads[2:]:
         load.wait()
 
@@ -199,7 +196,7 @@
         return jnp.concatenate([ref[gi, :, h * HD : (h + 1) * HD] for h in range(first, first + count)], axis=0)
 
     def key_rows(i, gi, j):
-        return kv_all[i, j, :, gi * HD : (gi + 1) * HD].astype(bf16)
+        return kv_all[i, gi, j].astype(bf16)
 
     def scores(keys, queries, j):
         raw = lax.dot_general(keys, queries, NT, preferred_element_type=f32)
@@ -222,9 +219,10 @@
                 values, head_rows(go_s, gi, n * unit, unit), NT, preferred_element_type=f32
             )
 
-    forward(0)
-    collect(0)
+        forward(0, gi)
+
     for gi in range(groups):
+        collect(0, gi)
         keys = [key_rows(0, gi, j) for j in range(V)]
         for n in range(units):
             there = unit_columns(n)
@@ -248,11 +246,10 @@
                 tick()
         grad = jnp.dot(p_all[gi], head_rows(go_s, gi, 0, gheads), preferred_element_type=f32)
         launch(gi, grad)
-        if gi == 0:
-            forward(1)
-
-    collect(1)
+        forward(1, gi)
+
     for gi in range(groups):
+        collect(1, gi)
         values = [key_rows(1, gi, j) for j in range(V)]
         for n in range(units):
             there = unit_columns(n)
@@ -275,8 +272,8 @@
 
     outs = []
     for gi in range(groups):
-        kt = jnp.concatenate([kv_all[0, j, :, gi * HD : (gi + 1) * HD].T for j in range(V)], axis=1).astype(bf16)
-        vt = jnp.concatenate([kv_all[1, j, :, gi * HD : (gi + 1) * HD].T for j in range(V)], axis=1).astype(bf16)
+        kt = jnp.concatenate([kv_all[0, gi, j].T for j in range(V)], axis=1).astype(bf16)
+        vt = jnp.concatenate([kv_all[1, gi, j].T for j in range(V)], axis=1).astype(bf16)
         for n in range(units):
             there = unit_columns(n)
             out = jnp.dot(vt, p_all[gi, :, there], preferred_element_type=f32)
@@ -309,7 +306,7 @@
         there = slice(g * HD, (g + 1) * HD)
         dv_ref[:, there] = sum(r_z[gi, k, rank] for gi, rank in found for k in range(Z)).astype(bf16)
         dk_ref[:, there] = sum(r_z[groups + gi, k, rank] for gi, rank in found for k in range(Z)).astype(bf16)
-    for copy in pending + sends[0] + sends[1] + forwards[0] + forwards[1]:
+    for copy in pending + list(sends.values()) + list(forwards.values()):
         copy.wait_send()
     for copy in outs:
         copy.wait()
@@ -332,7 +329,6 @@
     heads = H // V
     groups = max(1, heads // PER_GROUP)
     gheads = heads // groups
-    gw = groups * HD
     R = own // T
     f32, bf16 = jnp.float32, jnp.bfloat16
     dma = pltpu.SemaphoreType.DMA
@@ -344,9 +340,9 @@
         pltpu.VMEM((groups, rows, gheads * HD), bf16),
         pltpu.VMEM((groups, rows, gheads * HD), bf16),
         pltpu.VMEM((2, own, G * HD), bf16),
-        pltpu.VMEM((2, V - 1, own // CORES, gw), f32),
-        pltpu.VMEM((2, V - 1, CORES, own // CORES, gw), f32),
-        pltpu.VMEM((2, V, own, gw), f32),
+        pltpu.VMEM((2, groups, V - 1, own // CORES, HD), f32),
+        pltpu.VMEM((2, groups, V - 1, CORES, own // CORES, HD), f32),
+        pltpu.VMEM((2, groups, V, own, HD), f32),
         pltpu.VMEM((V, own, rows), f32),
         pltpu.VMEM((groups, V, own, gheads * rows), f32),
         pltpu.VMEM((groups, own, gheads * rows), f32),
@@ -365,7 +361,7 @@
         pltpu.VMEM((groups, rows, gheads * HD), bf16),
         dma((2 + 2 * groups,)),
         dma((groups, 2)),
-        dma((2, V - 1)), dma((2, V - 1)), dma((2, V - 1)), dma((2, V - 1)),
+        dma((2, groups, V - 1)), dma((2, groups, V - 1)), dma((2, groups, V - 1)), dma((2, groups, V - 1)),
         dma((pieces,)), dma((pieces,)),
         dma((pieces, Y - 1)), dma((pieces, Y - 1)),
         dma((pieces, Z * V - 1)), dma((pieces, Z * V - 1)),
@@ -398,6 +394,7 @@
         in_specs=[hbm] * 4,
         out_specs=(hbm,) * 4,
         scratch_shapes=[dma((4,))],
+        compiler_params=pltpu.CompilerParams(vmem_limit_bytes=1024 * 1024),
         name="hand_on",
     )(*results)
 

time: 67.8 us -> 31.4 us (0.46)
  Pallas kernels: 64.2 us -> 30.6 us
  local copies, waits for them, and re-layouts: 2.78 us -> 0 us
    pallas_call x1, Pallas kernels: 33.9 us -> 1.01 us  [local(): pl.pallas_call(hand_on, out_shape=shapes, in_specs=[hbm] * 4, out_specs=(...]
    unnamed x8 -> x0, local copies, waits for them, and re-layouts: 2.78 us -> none
    pallas_call x1, Pallas kernels: 30.3 us -> 29.6 us  [local(): pl.pallas_call(functools.partial(kernel, T, V), out_shape=tuple((pltpu.VM...]
where the time goes in v6:
time: 31.4 us; the launch traced here: 31.2 us
  Pallas kernels  30.6 us (97%)
  between operations  0.64 us (2%)
    pallas_call x1, Pallas kernels, local(): pl.pallas_call(functools.partial(kernel, T, V), out_shape=tuple((pltpu.VM...  29.6 us
    pallas_call x1, Pallas kernels, local(): pl.pallas_call(hand_on, out_shape=shapes, in_specs=[hbm] * 4, out_specs=(...  1.01 us

profile of v6, /device:TPU:0, one launch (start us, length us, event | category | flops | bytes accessed | tf_op | source)
XLA Modules:
  0.0 31.2 jit_solution(14123281856569665561)
XLA Ops:
  0.6 29.6 %attention.1 = (bf16[128,2048]{1,0:T(8,128)(2,1)S(1)}, bf16[128,2048]{1,0:T(8,128)(2,1)S(1)}, bf16[16,512]{1,0:T(8,128)(2,1)S(1)}, bf16[16,512]{1,0:T(8,128)(2,1)S(1)}) custom-call(bf16[128,4096]{1,0:T(8,128)(2,1)} %q_ref.1, bf16[128,4096]{1,0:T(8,128)(2,1)} %go_ref.1, bf16[256,512]{1,0:T(8,128)(2,1)} %k_ref.1, bf16[256,512]{1,0:T(8,128)(2,1)} %v_ref.1, ...), custom_call_target="tpu_custom_call" | custom-call | flops 1610612736 | bytes 2621440 | tf_op jit(solution)/shard_map/attention/pallas_call | solution.py:375
  30.2 1.0 %hand_on.1 = (bf16[128,2048]{1,0:T(8,128)(2,1)}, bf16[128,2048]{1,0:T(8,128)(2,1)}, bf16[16,512]{1,0:T(8,128)(2,1)}, bf16[16,512]{1,0:T(8,128)(2,1)}) custom-call(bf16[128,2048]{1,0:T(8,128)(2,1)S(1)} %get-tuple-element.8.refs_0_, bf16[128,2048]{1,0:T(8,128)(2,1)S(1)} %get-tuple-element.9.refs_1_, bf16[16,512]{1,0:T(8,128)(2,1)S(1)} %get-tuple-element.10.refs_2_, ...), custom_call_target="tpu_custom_call" | custom-call | tf_op jit(solution)/shard_map/hand_on/pallas_call | solution.py:391

commit v7 on v6

--- a/solution.py
+++ b/solution.py
@@ -224,6 +224,7 @@
     for gi in range(groups):
         collect(0, gi)
         keys = [key_rows(0, gi, j) for j in range(V)]
+        grad = jnp.zeros((V * own, HD), f32)
         for n in range(units):
             there = unit_columns(n)
             queries = head_rows(q_s, gi, n * unit, unit)
@@ -242,15 +243,15 @@
                 weight = shrink[j] * inverse
                 weights[gi, j, :, there] = weight
                 p_all[gi, j * own : (j + 1) * own, there] = (e[j] * weight).astype(bf16)
-            if n == 0:
-                tick()
-        grad = jnp.dot(p_all[gi], head_rows(go_s, gi, 0, gheads), preferred_element_type=f32)
+            grad += jnp.dot(p_all[gi, :, there], head_rows(go_s, gi, n * unit, unit), preferred_element_type=f32)
+        tick()
         launch(gi, grad)
         forward(1, gi)
 
     for gi in range(groups):
         collect(1, gi)
         values = [key_rows(1, gi, j) for j in range(V)]
+        grad = jnp.zeros((V * own, HD), f32)
         for n in range(units):
             there = unit_columns(n)
             gp = head_rows(go_s, gi, n * unit, unit)
@@ -265,10 +266,9 @@
                 ds_all[gi, j * own : (j + 1) * own, there] = (
                     s_all[gi, j, :, there] * ((dprob[j] - delta) * weight[j])
                 ).astype(bf16)
-            if n == 0:
-                tick()
-        grad = jnp.dot(ds_all[gi], head_rows(q_s, gi, 0, gheads), preferred_element_type=f32) * scale
-        launch(groups + gi, grad)
+            grad += jnp.dot(ds_all[gi, :, there], head_rows(q_s, gi, n * unit, unit), preferred_element_type=f32)
+        tick()
+        launch(groups + gi, grad * scale)
 
     outs = []
     for gi in range(groups):

time: 31.4 us -> 30.3 us (0.965)
  Pallas kernels: 30.6 us -> 29.5 us
    pallas_call x1, Pallas kernels: 29.6 us -> 28.5 us  [local(): pl.pallas_call(functools.partial(kernel, T, V), out_shape=tuple((pltpu.VM...]
where the time goes in v7:
time: 30.3 us; the launch traced here: 30.2 us
  Pallas kernels  29.5 us (97%)
  between operations  0.64 us (2%)
    pallas_call x1, Pallas kernels, local(): pl.pallas_call(functools.partial(kernel, T, V), out_shape=tuple((pltpu.VM...  28.5 us
    pallas_call x1, Pallas kernels, local(): pl.pallas_call(hand_on, out_shape=shapes, in_specs=[hbm] * 4, out_specs=(...  1.01 us

profile of v7, /device:TPU:0, one launch (start us, length us, event | category | flops | bytes accessed | tf_op | source)
XLA Modules:
  0.0 30.2 jit_solution(8933098753532469472)
XLA Ops:
  0.6 28.5 %attention.1 = (bf16[128,2048]{1,0:T(8,128)(2,1)S(1)}, bf16[128,2048]{1,0:T(8,128)(2,1)S(1)}, bf16[16,512]{1,0:T(8,128)(2,1)S(1)}, bf16[16,512]{1,0:T(8,128)(2,1)S(1)}) custom-call(bf16[128,4096]{1,0:T(8,128)(2,1)} %q_ref.1, bf16[128,4096]{1,0:T(8,128)(2,1)} %go_ref.1, bf16[256,512]{1,0:T(8,128)(2,1)} %k_ref.1, bf16[256,512]{1,0:T(8,128)(2,1)} %v_ref.1, ...), custom_call_target="tpu_custom_call" | custom-call | flops 1610612736 | bytes 2621440 | tf_op jit(solution)/shard_map/attention/pallas_call | solution.py:375
  29.2 1.0 %hand_on.1 = (bf16[128,2048]{1,0:T(8,128)(2,1)}, bf16[128,2048]{1,0:T(8,128)(2,1)}, bf16[16,512]{1,0:T(8,128)(2,1)}, bf16[16,512]{1,0:T(8,128)(2,1)}) custom-call(bf16[128,2048]{1,0:T(8,128)(2,1)S(1)} %get-tuple-element.8.refs_0_, bf16[128,2048]{1,0:T(8,128)(2,1)S(1)} %get-tuple-element.9.refs_1_, bf16[16,512]{1,0:T(8,128)(2,1)S(1)} %get-tuple-element.10.refs_2_, ...), custom_call_target="tpu_custom_call" | custom-call | tf_op jit(solution)/shard_map/hand_on/pallas_call | solution.py:391

commit v8 on v7

--- a/solution.py
+++ b/solution.py
@@ -166,13 +166,25 @@
                         part[p, cc, yy, zz, source(j)] = grad[at : at + R]
         flying.append([p, 0, start_core(p)])
 
+    def advance(piece):
+        p, stage, copies = piece
+        if stage < len(stages):
+            pending.extend(copies)
+            piece[2] = stages[stage](p, copies)
+            piece[1] = stage + 1
+
     def tick():
         for piece in reversed(flying):
-            p, stage, copies = piece
-            if stage < len(stages):
-                pending.extend(copies)
-                piece[2] = stages[stage](p, copies)
-                piece[1] = stage + 1
+            advance(piece)
+
+    def launch_between(p, grad):
+        fresh = [piece for piece in flying if piece[1] == 0]
+        older = [piece for piece in flying if piece[1] == 1]
+        for piece in fresh:
+            advance(piece)
+        launch(p, grad)
+        for piece in older:
+            advance(piece)
 
     pos = pos_ref[...]
     low = span_ref[0, 0]
@@ -244,8 +256,7 @@
                 weights[gi, j, :, there] = weight
                 p_all[gi, j * own : (j + 1) * own, there] = (e[j] * weight).astype(bf16)
             grad += jnp.dot(p_all[gi, :, there], head_rows(go_s, gi, n * unit, unit), preferred_element_type=f32)
-        tick()
-        launch(gi, grad)
+        launch_between(gi, grad)
         forward(1, gi)
 
     for gi in range(groups):
@@ -267,8 +278,7 @@
                     s_all[gi, j, :, there] * ((dprob[j] - delta) * weight[j])
                 ).astype(bf16)
             grad += jnp.dot(ds_all[gi, :, there], head_rows(q_s, gi, n * unit, unit), preferred_element_type=f32)
-        tick()
-        launch(groups + gi, grad * scale)
+        launch_between(groups + gi, grad * scale)
 
     outs = []
     for gi in range(groups):

time: 30.3 us -> 30.1 us (level)
  no operation moved by 1% of the time
where the time goes in v8:
time: 30.1 us; the launch traced here: 30 us
  Pallas kernels  29.3 us (97%)
  between operations  0.64 us (2%)
    pallas_call x1, Pallas kernels, local(): pl.pallas_call(functools.partial(kernel, T, V), out_shape=tuple((pltpu.VM...  28.3 us
    pallas_call x1, Pallas kernels, local(): pl.pallas_call(hand_on, out_shape=shapes, in_specs=[hbm] * 4, out_specs=(...  1.01 us

profile of v8, /device:TPU:0, one launch (start us, length us, event | category | flops | bytes accessed | tf_op | source)
XLA Modules:
  0.0 30.0 jit_solution(15086121301825559458)
XLA Ops:
  0.6 28.3 %attention.1 = (bf16[128,2048]{1,0:T(8,128)(2,1)S(1)}, bf16[128,2048]{1,0:T(8,128)(2,1)S(1)}, bf16[16,512]{1,0:T(8,128)(2,1)S(1)}, bf16[16,512]{1,0:T(8,128)(2,1)S(1)}) custom-call(bf16[128,4096]{1,0:T(8,128)(2,1)} %q_ref.1, bf16[128,4096]{1,0:T(8,128)(2,1)} %go_ref.1, bf16[256,512]{1,0:T(8,128)(2,1)} %k_ref.1, bf16[256,512]{1,0:T(8,128)(2,1)} %v_ref.1, ...), custom_call_target="tpu_custom_call" | custom-call | flops 1610612736 | bytes 2621440 | tf_op jit(solution)/shard_map/attention/pallas_call | solution.py:385
  28.9 1.0 %hand_on.1 = (bf16[128,2048]{1,0:T(8,128)(2,1)}, bf16[128,2048]{1,0:T(8,128)(2,1)}, bf16[16,512]{1,0:T(8,128)(2,1)}, bf16[16,512]{1,0:T(8,128)(2,1)}) custom-call(bf16[128,2048]{1,0:T(8,128)(2,1)S(1)} %get-tuple-element.8.refs_0_, bf16[128,2048]{1,0:T(8,128)(2,1)S(1)} %get-tuple-element.9.refs_1_, bf16[16,512]{1,0:T(8,128)(2,1)S(1)} %get-tuple-element.10.refs_2_, ...), custom_call_target="tpu_custom_call" | custom-call | tf_op jit(solution)/shard_map/hand_on/pallas_call | solution.py:401
